TPU v7x, 256 devices: a whole 4x4x8 slice. The times are simulated.
256 devices in a mesh: ctx: 64 (over x, y_lo, z), head: 4 (over y_hi, core).
Axes of the slice: x: 4, y: 4 (y_hi: 2, y_lo: 2; y = y_hi * 2 + y_lo), z: 8, core: 2. Of those that a mesh axis runs over, the one named last changes fastest.
Arguments:
- query: bfloat16 [16384, 2048], P('ctx', 'head'), may hold values from -8 to 8
- keys: bfloat16 [16384, 512], P('ctx', 'head'), may hold values from -6 to 6
- values: bfloat16 [16384, 512], P('ctx', 'head'), may hold values from -6 to 6
- out_weight: bfloat16 [2048, 4096], P('head'), may hold values from -0.125 to 0.125
Outputs:
- projected: bfloat16 [16384, 4096], P('ctx', 'head')
All inputs are finite; a program needn't handle non-finite values.
Results may differ from a plain program's by a relative error of at most 0.015.
Values may be sent and summed in bfloat16 or wider, within the bound.
A program may use at most 192 MiB of HBM per device.

v0:
```python
import math

import jax
import jax.numpy as jnp
from jax import lax
from jax.sharding import PartitionSpec as P

HD = 128


def absorb(state, q_rows, q_pos, k_piece, v_piece, k_pos, scale):
    running, summed, accum = state
    scores = (
        jnp.einsum("tkgd,skd->kgts", q_rows, k_piece, preferred_element_type=jnp.float32) * scale
    )
    allowed = k_pos[None, :] <= q_pos[:, None]
    fresh = jnp.maximum(running, jnp.max(jnp.where(allowed, scores, -1e30), axis=-1))
    weights = jnp.where(allowed, jnp.exp(scores - fresh[..., None]), 0.0)
    summed = jnp.sum(weights, axis=-1)
    accum = jnp.einsum(
        "kgts,skd->kgtd", weights.astype(jnp.bfloat16), v_piece, preferred_element_type=jnp.float32
    )
    return (fresh, summed, accum)


def empty_state(kv_local, group, count):
    return (
        jnp.full((kv_local, group, count), -1e30, jnp.float32),
        jnp.zeros((kv_local, group, count), jnp.float32),
        jnp.zeros((kv_local, group, count, HD), jnp.float32),
    )


def per_device(query, keys, values, out_weight):
    rows = query.shape[0]
    kv_local = keys.shape[1] // HD
    q_local = query.shape[1] // HD
    group = q_local // kv_local
    me = lax.axis_index("ctx")
    scale = 1.0 / math.sqrt(HD)
    local_iota = jnp.arange(rows, dtype=jnp.int32)
    q_rows = query.reshape(rows, kv_local, group, HD)
    q_pos = me * rows + local_iota
    newest = me * rows + rows - 1
    init = empty_state(kv_local, group, rows)
    k_piece = lax.all_gather(keys, "ctx", axis=0, tiled=True)
    v_piece = lax.all_gather(values, "ctx", axis=0, tiled=True)
    count = k_piece.shape[0]
    k_three = k_piece.reshape(count, kv_local, HD)
    v_three = v_piece.reshape(count, kv_local, HD)
    k_pos = jnp.arange(count, dtype=jnp.int32)

    def work(inner):
        return absorb(inner, q_rows, q_pos, k_three, v_three, k_pos, scale)

    def keep(inner):
        return inner

    result = lax.cond(jnp.int32(0) <= newest, work, keep, init)
    summed = result[1]
    accum = result[2]
    mixed = accum / summed[..., None]
    attended = jnp.transpose(mixed, (2, 0, 1, 3)).reshape(rows, q_local * HD).astype(jnp.bfloat16)
    partial_sum = jnp.dot(attended, out_weight, preferred_element_type=jnp.float32)
    return lax.psum_scatter(
        partial_sum.astype(jnp.bfloat16), "head", scatter_dimension=1, tiled=True
    )


def solution(mesh):
    return jax.shard_map(
        per_device,
        mesh=mesh,
        in_specs=(P("ctx", "head"), P("ctx", "head"), P("ctx", "head"), P("head", None)),
        out_specs=P("ctx", "head"),
        check_vma=False,
    )
```

profile of v0, /device:TPU:3, one launch (start us, length us, event | category | flops | bytes accessed | tf_op | source)
XLA Modules:
  0.0 755.9 jit_solution(307988265351984877)
XLA Ops:
  6.5 0.0 all-gather.3.cloned.1.call-start
  6.5 0.7 all-gather.3.cloned.1.call-update
  7.3 0.0 all-gather.5.cloned.1.call-start
  7.3 0.7 all-gather.5.cloned.1.call-update
  8.0 0.0 reduce-scatter.2.cloned.1.call-start
  8.1 241.9 %all-gather.3.cloned.1.call-done = bf16[16384,128]{1,0:T(8,128)(2,1)} async-done(((bf16[256,128]{1,0:T(8,128)(2,1)}), bf16[16384,128]{1,0:T(8,128)(2,1)}) %all-gather.3.cloned.1.call-update) | async-done | bytes 4194320 | tf_op jit(solution)/shard_map/all_gather | solution.py:46
  250.0 302.9 %all-gather.5.cloned.1.call-done = bf16[16384,128]{1,0:T(8,128)(2,1)} async-done(((bf16[256,128]{1,0:T(8,128)(2,1)}), bf16[16384,128]{1,0:T(8,128)(2,1)}) %all-gather.5.cloned.1.call-update) | async-done | bytes 4194320 | tf_op jit(solution)/shard_map/all_gather | solution.py:47
  552.9 84.6 %conditional.1 = (f32[1,4,256]{2,1,0:T(4,128)S(1)}, f32[1,4,256,128]{2,3,1,0:T(8,128)S(1)}) conditional(s32[]{:T(128)} %convert_element_type.18, () %tuple.13, (s32[16384]{0:T(1024)S(1)}, s32[]{:T(128)}, s32[256]{0:T(256)S(1)}, bf16[256,512]{1,0:T(8,128)(2,1)}, bf16[16384,128]{1,0:T(8,128)(2,1)}, /*index=5*/bf16[16384,128]{1,0:T(8,128)(2,1)}) %tuple.14), branch_computations={%region_0.0_spmd, %region_1.4_spmd} | conditional | flops 8778677248 | bytes 227372048 | solution.py:59
  552.9 8.2 %broadcast_compare_fusion = pred[256,16384]{0,1:T(8,128)(4,1)} fusion(s32[256]{0:T(256)S(1)} %broadcast_add_fusion, s32[16384]{0:T(1024)S(1)} %get-tuple-element.22), kind=kLoop, calls=%fused_computation.10 | loop fusion | flops 4194304 | bytes 4260864 | tf_op jit(solution)/shard_map/cond/branch_1_fun/le | solution.py:16
  561.1 27.3 %fusion = (f32[4,256]{1,0:T(4,128)S(1)}, f32[16384,256,4]{1,0,2:T(8,128)}) fusion(pred[256,16384]{0,1:T(8,128)(4,1)} %broadcast_compare_fusion, bf16[16384,128]{1,0:T(8,128)(2,1)} %get-tuple-element.25, bf16[256,512]{1,0:T(8,128)(2,1)} %get-tuple-element.33), kind=kOutput, calls=%fused_computation.2 | convolution fusion | flops 4345297920 | bytes 75763712 | tf_op jit(solution)/shard_map/cond/branch_1_fun/tkgd,skd->kgts/dot_general | solution.py:14
  588.4 26.4 %fusion.12 = f32[1,4,256,128]{2,3,1,0:T(8,128)S(1)} fusion(bf16[16384,128]{1,0:T(8,128)(2,1)} %get-tuple-element.27, f32[16384,256,4]{1,0,2:T(8,128)} %get-tuple-element.36, f32[4,256]{1,0:T(4,128)S(1)} %broadcast_maximum_fusion, pred[256,16384]{0,1:T(8,128)(4,1)} %broadcast_compare_fusion), kind=kOutput, calls=%fused_computation.14 | convolution fusion | flops 4362076160 | bytes 76025856 | tf_op jit(solution)/shard_map/cond/branch_1_fun/kgts,skd->kgtd/dot_general | solution.py:20
  614.8 22.7 %fusion.4 = f32[4,256]{1,0:T(4,128)S(1)} fusion(f32[16384,256,4]{1,0,2:T(8,128)} %get-tuple-element.36, f32[4,256]{1,0:T(4,128)S(1)} %broadcast_maximum_fusion, pred[256,16384]{0,1:T(8,128)(4,1)} %broadcast_compare_fusion), kind=kLoop, calls=%fused_computation.6 | loop fusion | flops 67107840 | bytes 71311360 | tf_op jit(solution)/shard_map/cond/branch_1_fun/reduce_sum | solution.py:19
  637.5 4.8 convolution_convert_fusion
  642.3 0.0 reduce-scatter.2.cloned.1.call-update
  642.4 107.0 %reduce-scatter.2.cloned.1.call-done = bf16[256,1024]{1,0:T(8,128)(2,1)} async-done(((bf16[256,4096]{1,0:T(8,128)(2,1)}), bf16[256,1024]{1,0:T(8,128)(2,1)}) %reduce-scatter.2.cloned.1.call-update) | async-done | bytes 524304 | tf_op jit(solution)/shard_map/reduce_scatter | solution.py:65
  (5 shorter events, 0.1 us)
Async XLA Ops:
  6.5 243.4 %all-gather.3.cloned.1.call-start = ((), (), s32[]{:S(2)}) async-start(), calls=%async_computation.1 | async-start | bytes 4259840 | tf_op jit(solution)/shard_map/all_gather | solution.py:46
  7.3 545.6 %all-gather.5.cloned.1.call-start = ((), (), s32[]{:S(2)}) async-start(), calls=%async_computation.2 | async-start | bytes 4259840 | tf_op jit(solution)/shard_map/all_gather | solution.py:47
  8.0 741.3 %reduce-scatter.2.cloned.1.call-start = ((), (), s32[]{:S(2)}) async-start(), calls=%async_computation.3 | async-start | bytes 2621440 | tf_op jit(solution)/shard_map/reduce_scatter | solution.py:65
Sparse Core Ops, SparseCore 0:
  9.1 240.7 all-gather.2
  251.7 301.0 all-gather.4
  642.5 106.7 reduce-scatter.1
where the time goes:
time: 757 us; the launch traced here: 756 us
  waiting for transfers between devices  653 us (86%)
  matrix products  58.4 us (8%)
  other arithmetic  31 us (4%)
  between operations  13.1 us (2%)
    all_gather x1, waiting for transfers between devices, per_device(): v_piece = lax.all_gather(values, 'ctx', axis=0, tiled=True)  303 us
    all_gather x1, waiting for transfers between devices, per_device(): k_piece = lax.all_gather(keys, 'ctx', axis=0, tiled=True)  242 us
    reduce_scatter x1, waiting for transfers between devices, per_device(): lax.psum_scatter(partial_sum.astype(jnp.bfloat16), 'head', scatter_dimens...  107 us
    dot_general x1, matrix products, absorb(): jnp.einsum('tkgd,skd->kgts', q_rows, k_piece, preferred_element_type=jnp....  27.3 us
    dot_general x1, matrix products, absorb(): jnp.einsum('kgts,skd->kgtd', weights.astype(jnp.bfloat16), v_piece, prefe...  26.4 us
    reduce_sum x1, other arithmetic, absorb(): summed = jnp.sum(weights, axis=-1)  22.7 us
  transfers between devices with their start and end apart: 3, of which 3 were waited for; matrix products, arithmetic and copies ran while one was open for 0% of the time, Pallas kernels for 0%

commit v1 on v0

v1 whole, which is shorter than its diff:
```python
import functools
import math

import jax
import jax.numpy as jnp
from jax import lax
from jax.experimental import pallas as pl
from jax.experimental.pallas import tpu as pltpu
from jax.sharding import PartitionSpec as P

HD = 128
ROWS = 256
NX, NZ = 4, 8
NU = 2 * NX
LOG2E = math.log2(math.e)
FLOOR = -1e30
PEN = 1e32
WCH = 4
MESH = pl.DeviceIdType.MESH
BF = jnp.bfloat16
F32 = jnp.float32


def dev(x, yl, z, yh, c):
    return {"ctx": (x * 2 + yl) * NZ + z, "head": yh * 2 + c}


def kernel(
    q_ref, k_ref, v_ref, w_ref, o_ref,
    vst, kvbuf, qbuf, s_ref, mx_ref, acc, m_ref, l_ref,
    osend, ssend, orecv, srecv, attsend, att, wbuf,
    sw_s, sw_r, qs_s, qs_r, z_s, z_r, sib_s, sib_r,
    w1_s, w1_r, w2_s, w2_r, w3_s, w3_r, wl,
    os_s, os_r, at_s, at_r, as_s, as_r,
):
    ctx = lax.axis_index("ctx")
    head = lax.axis_index("head")
    x = ctx // (2 * NZ)
    yl = (ctx // NZ) % 2
    z = ctx % NZ
    yh = head // 2
    c = head % 2
    scale = LOG2E / math.sqrt(HD)
    D = functools.partial(dev)
    zp, zm = (z + 1) % NZ, (z + NZ - 1) % NZ

    barrier = pltpu.get_barrier_semaphore()
    partners = []
    for i in range(1, 8):
        a, b, d = i // 4, (i // 2) % 2, i % 2
        partners.append(D(x, (yl + b) % 2, z, (yh + a) % 2, (c + d) % 2))
    for i in range(1, NX):
        partners.append(D((x + i) % NX, yl, z, yh, c))
    partners += [D(x, yl, zp, yh, c), D(x, yl, zm, yh, c)]
    for p in partners:
        pl.semaphore_signal(barrier, inc=1, device_id=p, device_id_type=MESH)
    vst[0:HD, :] = v_ref[0:HD, :].T
    vst[HD:ROWS, :] = v_ref[HD:ROWS, :].T
    pl.semaphore_wait(barrier, len(partners))

    def rcopy(src, dst, ss, rs, to):
        return pltpu.make_async_remote_copy(
            src_ref=src, dst_ref=dst, send_sem=ss, recv_sem=rs, device_id=to, device_id_type=MESH
        )

    sib = D(x, yl, z, yh, 1 - c)
    lo, hi = 2 * x, 2 * x + 1

    swap_to = D(x, c, z, yh, yl)
    away = c != yl

    def kv_half(slot, zz, half):
        return kvbuf.at[slot, zz, pl.ds(half * ROWS, ROWS), :]

    def q_to(d):
        return D(x, c, z, yh, d)

    def q_src(d):
        return q_ref.at[:, pl.ds(d * 2 * HD, 2 * HD)]

    kcp = rcopy(k_ref, kv_half(yl, z, 0), sw_s.at[0], sw_r.at[0], swap_to)
    vcp = rcopy(vst, kv_half(yl, z, 1), sw_s.at[1], sw_r.at[1], swap_to)
    klc = pltpu.make_async_copy(k_ref, kv_half(yl, z, 0), sw_r.at[0])
    vlc = pltpu.make_async_copy(vst, kv_half(yl, z, 1), sw_r.at[1])

    def q_remote(d):
        return rcopy(q_src(d), qbuf.at[2 * x + yl], sw_s.at[2 + d], qs_r.at[2 * x + yl], q_to(d))

    def q_local(d):
        return pltpu.make_async_copy(q_src(d), qbuf.at[2 * x + yl], qs_r.at[2 * x + yl])

    @pl.when(away)
    def _():
        kcp.start()
        vcp.start()
        for d in range(2):
            q_remote(d).start()

    @pl.when(jnp.logical_not(away))
    def _():
        klc.start()
        vlc.start()
        for d in range(2):
            @pl.when(c == d)
            def _():
                q_local(d).start()

            @pl.when(c != d)
            def _():
                q_remote(d).start()

    DC = o_ref.shape[1]
    WR = w_ref.shape[0]
    WP = WR // WCH
    gw = yh * 2 + c
    xrow = (1 - yh) * 2 + yl
    yrow = (1 - yh) * 2 + (1 - yl)

    def w1(j, d):
        return rcopy(
            w_ref.at[pl.ds(j * WP, WP), pl.ds(((1 - yh) * 2 + d) * DC, DC)],
            wbuf.at[gw, pl.ds(j * WP, WP), :],
            w1_s.at[j, d], w1_r.at[j], D(x, 1 - yl, z, 1 - yh, d),
        )

    def w1_in(j):
        return rcopy(
            wbuf.at[xrow, pl.ds(j * WP, WP), :], wbuf.at[xrow, pl.ds(j * WP, WP), :],
            w2_s.at[j], w1_r.at[j], D(x, 1 - yl, z, yh, c),
        )

    def w2(j):
        return rcopy(
            wbuf.at[xrow, pl.ds(j * WP, WP), :], wbuf.at[xrow, pl.ds(j * WP, WP), :],
            w2_s.at[j], w2_r.at[j], D(x, 1 - yl, z, yh, c),
        )

    w3 = rcopy(
        w_ref.at[:, pl.ds((yh * 2 + 1 - c) * DC, DC)], wbuf.at[gw], w3_s, w3_r, sib
    )
    wown = pltpu.make_async_copy(w_ref.at[:, pl.ds(gw * DC, DC)], wbuf.at[gw], wl)

    def blk(slot, zz):
        return kvbuf.at[slot, zz]

    def zfwd(zz, d, n, to):
        return rcopy(blk(c, zz), blk(c, zz), z_s.at[d, n], z_r.at[d, n], to)

    zup, zdn = D(x, yl, zp, yh, c), D(x, yl, zm, yh, c)
    rel = [z, zm, zp, (z + NZ - 2) % NZ, (z + 2) % NZ, (z + NZ - 3) % NZ, (z + 3) % NZ,
           (z + NZ - 4) % NZ]

    def up(n, r):
        return zfwd(rel[r], 0, n, zup)

    def down(n, r):
        return zfwd(rel[r], 1, n, zdn)

    def tosib(r):
        return rcopy(blk(c, rel[r]), blk(c, rel[r]), sib_s.at[r], sib_r.at[r], sib)

    def arrive(r):
        k = (r + 1) // 2
        if r % 2 == 1:
            zfwd(rel[r], 0, k - 1, zup).wait_recv()
        else:
            zfwd(rel[r], 1, k - 1, zdn).wait_recv()
        if r % 2 == 1 and k < 4:
            up(k, r).start()
        if r % 2 == 0 and k < 3:
            down(k, r).start()
        tosib(r).start()

    def sib_arrive(r):
        rcopy(blk(1 - c, rel[r]), blk(1 - c, rel[r]), sib_s.at[r], sib_r.at[r], sib).wait_recv()

    m_ref[...] = jnp.full_like(m_ref, FLOOR)
    l_ref[...] = jnp.zeros_like(l_ref)
    acc[...] = jnp.zeros_like(acc)

    for half in range(2):
        pltpu.make_async_copy(kv_half(c, z, half), kv_half(c, z, half), sw_r.at[half]).wait()
    up(0, 0).start()
    down(0, 0).start()
    tosib(0).start()

    @pl.when(c != yl)
    def _():
        for j in range(WCH):
            for d in range(2):
                w1(j, d).start()

    def q_wait(u):
        pltpu.make_async_copy(qbuf.at[u], qbuf.at[u], qs_r.at[u]).wait()

    q_wait(lo)
    q_wait(hi)

    def q_send(xt, s):
        u = 2 * x + s
        return rcopy(qbuf.at[u], qbuf.at[u], qs_s.at[xt, s], qs_r.at[u], D(xt, yl, z, yh, c))

    for xt in range(NX - 1):
        @pl.when(xt < x)
        def _():
            for s in range(2):
                q_send(xt, s).start()
    w3.start()
    wown.start()

    def hs(h):
        return slice(h * ROWS, (h + 1) * ROWS)

    def qk(slot, zz, u, h):
        return lax.dot_general(
            kvbuf[slot, zz, 0:ROWS, :], qbuf[u, :, h * HD:(h + 1) * HD],
            (((1,), (1,)), ((), ())), preferred_element_type=F32,
        )

    def vt(slot, zz):
        return jnp.concatenate(
            [kvbuf[slot, zz, ROWS:ROWS + HD, :], kvbuf[slot, zz, ROWS + HD:2 * ROWS, :]], axis=1
        )

    def pv(slot, zz, p):
        return lax.dot_general(
            vt(slot, zz), p.astype(BF), (((1,), (0,)), ((), ())), preferred_element_type=F32
        )

    def fold(a, op):
        return op(a.reshape(a.shape[0] // 8, 8, a.shape[1]), axis=0)

    def diagonal(slot, u):
        key_i = lax.broadcasted_iota(jnp.int32, (ROWS, ROWS), 0)
        qry_i = lax.broadcasted_iota(jnp.int32, (ROWS, ROWS), 1)
        allowed = key_i <= qry_i
        for h in range(2):
            s = jnp.where(allowed, qk(slot, z, u, h) * scale, -PEN)
            m = jnp.max(s, axis=0, keepdims=True)
            p = jnp.exp2(s - m)
            m_ref[u, 0:1, hs(h)] = m
            l_ref[u, :, hs(h)] = fold(p, jnp.sum)
            acc[u, :, hs(h)] = pv(slot, z, p)

    def pen(slot, zz, u):
        kid = (2 * x + slot) * NZ + zz
        return jnp.where(kid < u * NZ + z, 0.0, PEN).astype(F32)

    def score(slot, zs, u, h):
        mx = None
        for b in range(4):
            s = qk(slot, zs[b], u, h)
            s_ref[b * ROWS:(b + 1) * ROWS, hs(h)] = s
            top = fold(s, jnp.max) - pen(slot, zs[b], u)
            mx = top if mx is None else jnp.maximum(mx, top)
        mx_ref[:, hs(h)] = mx

    def absorb(slot, zs, u, un, h):
        m_old = m_ref[u, 0:1, hs(h)]
        m_new = jnp.maximum(m_old, jnp.max(mx_ref[:, hs(h)], axis=0, keepdims=True) * scale)
        alpha = jnp.exp2(m_old - m_new)
        m_ref[u, 0:1, hs(h)] = m_new
        l8, out = None, None
        for b in range(4):
            p = jnp.exp2(s_ref[b * ROWS:(b + 1) * ROWS, hs(h)] * scale - (m_new + pen(slot, zs[b], u)))
            p8 = fold(p, jnp.sum)
            l8 = p8 if l8 is None else l8 + p8
            d = pv(slot, zs[b], p)
            out = d if out is None else out + d
        score(slot, zs, un, h)
        l_ref[u, :, hs(h)] = l_ref[u, :, hs(h)] * alpha + l8
        acc[u, :, hs(h)] = acc[u, :, hs(h)] * alpha + out

    diagonal(c, 2 * x + c)
    arrive(1)
    arrive(2)
    sib_arrive(0)
    diagonal(1 - c, 2 * x + 1 - c)
    arrive(3)

    def o_send(u):
        return rcopy(osend.at[u], orecv.at[x, u % 2], os_s.at[u, 0], os_r.at[x, u % 2, 0],
                     D(u // 2, yl, z, yh, c))

    def st_send(u):
        return rcopy(ssend.at[u], srecv.at[x, u % 2], os_s.at[u, 1], os_r.at[x, u % 2, 1],
                     D(u // 2, yl, z, yh, c))

    def events(seg):
        if seg == 0:
            sib_arrive(1)
            sib_arrive(2)
            sib_arrive(3)
        if seg == 1:
            arrive(4)
        if seg == 3:
            arrive(5)
            arrive(6)
            w1_in(0).wait_recv()
            w2(0).start()
        if seg == 4:
            arrive(7)
            sib_arrive(4)
            sib_arrive(5)
            sib_arrive(6)
            sib_arrive(7)
        if seg in (5, 6, 7):
            w1_in(seg - 4).wait_recv()
            w2(seg - 4).start()

    def zsel(g):
        return [jnp.where(g == 0, rel[b], rel[b + 4]) for b in range(4)]

    def segment(seg, _):
        for e in range(8):
            if e != 2:
                pl.when(seg == e)(functools.partial(events, e))
        pss = seg // 2
        half = seg % 2
        slot = 1 - pss % 2
        zs = zsel(pss // 2)
        u0 = 2 * x + slot
        n = NU - u0
        mid = (n + 1) // 2
        last = pss == 3

        def at(i):
            return jnp.where(last, NU - 1 - i, u0 + i)

        @pl.when(half == 0)
        def _():
            for h in range(2):
                score(slot, zs, at(0), h)

        def one(i, _):
            u = at(i)
            un = at(jnp.minimum(i + 1, n - 1))

            @pl.when(jnp.logical_and(pss == 0, jnp.logical_and(un > u, un > hi)))
            def _():
                q_wait(un)

            for h in range(2):
                absorb(slot, zs, u, un, h)

            @pl.when(jnp.logical_and(last, u > hi))
            def _():
                osend[u] = acc[u].astype(BF)
                lsum = jnp.sum(l_ref[u], axis=0, keepdims=True)
                ssend[u] = jnp.concatenate(
                    [jnp.broadcast_to(m_ref[u, 0:1, :], (4, 2 * ROWS)),
                     jnp.broadcast_to(lsum, (4, 2 * ROWS))], axis=0)
                o_send(u).start()
                st_send(u).start()

            return 0

        lax.fori_loop(jnp.where(half == 0, 0, mid), jnp.where(half == 0, mid, n), one, 0)
        return 0

    lax.fori_loop(0, 8, segment, 0)

    for s in range(2):
        l_ref[2 * x + s] = jnp.broadcast_to(
            jnp.sum(l_ref[2 * x + s], axis=0, keepdims=True), (8, 2 * ROWS))

    def merge(xs, _):
        for s in range(2):
            u = 2 * x + s
            rcopy(osend.at[u], orecv.at[xs, s], os_s.at[u, 0], os_r.at[xs, s, 0], sib).wait_recv()
            rcopy(ssend.at[u], srecv.at[xs, s], os_s.at[u, 1], os_r.at[xs, s, 1], sib).wait_recv()
            m_old = m_ref[u, 0:1, :]
            m_in = srecv[xs, s, 0:1, :]
            m_new = jnp.maximum(m_old, m_in)
            a_old = jnp.exp2(m_old - m_new)
            a_in = jnp.exp2(m_in - m_new)
            m_ref[u, 0:1, :] = m_new
            l_ref[u, 0:1, :] = l_ref[u, 0:1, :] * a_old + srecv[xs, s, 4:5, :] * a_in
            acc[u] = acc[u] * a_old + orecv[xs, s].astype(F32) * a_in
        return 0

    lax.fori_loop(0, x, merge, 0)

    g = yh * 2 + yl

    def a_remote(s, t):
        return rcopy(attsend.at[s], att.at[g, c], at_s.at[s, t], at_r.at[g], D(x, s, z, t, c))

    def a_local(s):
        return pltpu.make_async_copy(attsend.at[s], att.at[g, c], at_r.at[g])

    for s in range(2):
        u = 2 * x + s
        for h in range(2):
            o = acc[u, :, hs(h)] / l_ref[u, 0:1, hs(h)]
            attsend[s, :, h * HD:(h + 1) * HD] = o.T.astype(BF)
        for t in range(2):
            here = jnp.logical_and(s == yl, t == yh)

            @pl.when(here)
            def _():
                a_local(s).start()

            @pl.when(jnp.logical_not(here))
            def _():
                a_remote(s, t).start()

    def a_sib(gg):
        return rcopy(att.at[gg, c], att.at[gg, c], as_s.at[gg], as_r.at[gg], sib)

    for gg in range(4):
        pltpu.make_async_copy(attsend.at[0], att.at[gg, c], at_r.at[gg]).wait()
        a_sib(gg).start()
    w3.wait_recv()
    wown.wait()
    for j in range(WCH):
        rcopy(wbuf.at[yrow, pl.ds(j * WP, WP), :], wbuf.at[yrow, pl.ds(j * WP, WP), :],
              w2_s.at[j], w2_r.at[j], sib).wait_recv()
    for gg in range(4):
        rcopy(att.at[gg, 1 - c], att.at[gg, 1 - c], as_s.at[gg], as_r.at[gg], sib).wait_recv()

    rows = jnp.concatenate([att[i // 2, i % 2] for i in range(8)], axis=1)
    for j in range(DC // 256):
        cs = slice(j * 256, (j + 1) * 256)
        wcol = jnp.concatenate([wbuf[i, :, cs] for i in range(4)], axis=0)
        o_ref[:, cs] = jnp.dot(rows, wcol, preferred_element_type=F32).astype(BF)

    @pl.when(away)
    def _():
        kcp.wait_send()
        vcp.wait_send()
        for d in range(2):
            q_remote(d).wait_send()

    @pl.when(jnp.logical_not(away))
    def _():
        for d in range(2):
            @pl.when(c != d)
            def _():
                q_remote(d).wait_send()

    @pl.when(c != yl)
    def _():
        for j in range(WCH):
            for d in range(2):
                w1(j, d).wait_send()
    for j in range(WCH):
        w2(j).wait_send()
    w3.wait_send()
    for n, r in ((0, 0), (1, 1), (2, 3), (3, 5)):
        up(n, r).wait_send()
    for n, r in ((0, 0), (1, 2), (2, 4)):
        down(n, r).wait_send()
    for r in range(8):
        tosib(r).wait_send()
    for xt in range(NX - 1):
        @pl.when(xt < x)
        def _():
            for s in range(2):
                q_send(xt, s).wait_send()

    def sent(u, _):
        o_send(u).wait_send()
        st_send(u).wait_send()
        return 0

    lax.fori_loop(2 * x + 2, NU, sent, 0)
    for s in range(2):
        for t in range(2):
            @pl.when(jnp.logical_not(jnp.logical_and(s == yl, t == yh)))
            def _():
                a_remote(s, t).wait_send()
    for gg in range(4):
        a_sib(gg).wait_send()


def per_device(query, keys, values, out_weight):
    rows = query.shape[0]
    d_model = out_weight.shape[1]
    dma = pltpu.SemaphoreType.DMA
    vm = pl.BlockSpec(memory_space=pltpu.VMEM)
    R2 = 2 * ROWS
    return pl.pallas_call(
        kernel,
        out_shape=jax.ShapeDtypeStruct((rows, d_model // 4), BF),
        in_specs=[vm, vm, vm, pl.BlockSpec(memory_space=pl.ANY)],
        out_specs=vm,
        scratch_shapes=[
            pltpu.VMEM((ROWS, HD), BF),
            pltpu.VMEM((2, NZ, R2, HD), BF),
            pltpu.VMEM((NU, ROWS, 2 * HD), BF),
            pltpu.VMEM((4 * ROWS, R2), F32),
            pltpu.VMEM((8, R2), F32),
            pltpu.VMEM((NU, HD, R2), F32),
            pltpu.VMEM((NU, 8, R2), F32),
            pltpu.VMEM((NU, 8, R2), F32),
            pltpu.VMEM((NU, HD, R2), BF),
            pltpu.VMEM((NU, 8, R2), F32),
            pltpu.VMEM((NX, 2, HD, R2), BF),
            pltpu.VMEM((NX, 2, 8, R2), F32),
            pltpu.VMEM((2, ROWS, 2 * HD), BF),
            pltpu.VMEM((4, 2, ROWS, 2 * HD), BF),
            pltpu.VMEM((4, out_weight.shape[0], d_model // 4), BF),
            dma((4,)), dma((2,)),
            dma((NX, 2)), dma((NU,)),
            dma((2, 4)), dma((2, 4)),
            dma((8,)), dma((8,)),
            dma((WCH, 2)), dma((WCH,)), dma((WCH,)), dma((WCH,)), dma, dma, dma,
            dma((NU, 2)), dma((NX, 2, 2)),
            dma((2, 2)), dma((4,)), dma((4,)), dma((4,)),
        ],
        compiler_params=pltpu.CompilerParams(
            collective_id=0, has_side_effects=True, vmem_limit_bytes=48 * 1024 * 1024
        ),
    )(query, keys, values, out_weight)


def solution(mesh):
    return jax.shard_map(
        per_device,
        mesh=mesh,
        in_specs=(P("ctx", "head"), P("ctx", "head"), P("ctx", "head"), P("head", None)),
        out_specs=P("ctx", "head"),
        check_vma=False,
    )
```

time: 757 us -> 78.6 us (0.10)
  waiting for transfers between devices: 653 us -> 0 us
  Pallas kernels: 0 us -> 72.2 us
  matrix products: 58.4 us -> 0 us
  other arithmetic: 31 us -> 0 us
  between operations: 13.1 us -> 0.01 us
    all_gather x2 -> x0, waiting for transfers between devices: 545 us -> none  [the longest x1 303 us: per_device(): v_piece = lax.all_gather(values, 'ctx', axis=0, tiled=True)]
    reduce_scatter x1 -> x0, waiting for transfers between devices: 107 us -> none  [per_device(): lax.psum_scatter(partial_sum.astype(jnp.bfloat16), 'head', scatter_dimens...]
    pallas_call x0 -> x1, Pallas kernels: none -> 72.2 us  [per_device(): pl.pallas_call(kernel, out_shape=jax.ShapeDtypeStruct((rows, d_model // 4...]
    dot_general x3 -> x0, matrix products: 58.4 us -> none  [the longest x1 27.3 us: absorb(): jnp.einsum('tkgd,skd->kgts', q_rows, k_piece, preferred_element_type=jnp....]
    reduce_sum x1 -> x0, other arithmetic: 22.7 us -> none  [absorb(): summed = jnp.sum(weights, axis=-1)]
    le x1 -> x0, other arithmetic: 8.21 us -> none  [absorb(): allowed = k_pos[None, :] <= q_pos[:, None]]
  transfers between devices with their start and end apart: 3 -> 0, of which waited for: 3 -> 0; matrix products, arithmetic and copies ran while one was open for 0% -> 0% of each run, Pallas kernels for 0% -> 0%
where the time goes in v1:
time: 78.6 us; the launch traced here: 77.8 us
  Pallas kernels  72.2 us (92%)
  local copies, waits for them, and re-layouts  5.61 us (7%)
    pallas_call x1, Pallas kernels, per_device(): pl.pallas_call(kernel, out_shape=jax.ShapeDtypeStruct((rows, d_model // 4...  72.2 us
    unnamed x9, local copies, waits for them, and re-layouts  5.61 us

profile of v1, /device:TPU:3, one launch (start us, length us, event | category | flops | bytes accessed | tf_op | source)
XLA Modules:
  0.0 77.8 jit_solution(8638293074156494086)
XLA Ops:
  0.0 0.0 copy-start
  0.0 2.2 %copy-done = bf16[512,4096]{1,0:T(8,128)(2,1)S(1)} copy-done((bf16[512,4096]{1,0:T(8,128)(2,1)S(1)}, bf16[512,4096]{1,0:T(8,128)(2,1)}, u32[]{:S(2)}) %copy-start) | copy-done | bytes 4194328
  2.2 0.0 copy-start.1
  2.2 0.9 %copy-done.1 = bf16[256,512]{1,0:T(8,128)(2,1)S(1)} copy-done((bf16[256,512]{1,0:T(8,128)(2,1)S(1)}, bf16[256,512]{1,0:T(8,128)(2,1)}, u32[]{:S(2)}) %copy-start.1) | copy-done | bytes 262168
  3.1 0.0 copy-start.2
  3.1 0.8 %copy-done.2 = bf16[256,128]{1,0:T(8,128)(2,1)S(1)} copy-done((bf16[256,128]{1,0:T(8,128)(2,1)S(1)}, bf16[256,128]{1,0:T(8,128)(2,1)}, u32[]{:S(2)}) %copy-start.2) | copy-done | bytes 65560
  4.0 0.0 copy-start.3
  4.0 0.8 %copy-done.3 = bf16[256,128]{1,0:T(8,128)(2,1)S(1)} copy-done((bf16[256,128]{1,0:T(8,128)(2,1)S(1)}, bf16[256,128]{1,0:T(8,128)(2,1)}, u32[]{:S(2)}) %copy-start.3) | copy-done | bytes 65560
  4.8 72.2 %shard_map.46 = bf16[256,1024]{1,0:T(8,128)(2,1)S(1)} custom-call(bf16[256,512]{1,0:T(8,128)(2,1)S(1)} %copy-done.1, bf16[256,128]{1,0:T(8,128)(2,1)S(1)} %copy-done.2, bf16[256,128]{1,0:T(8,128)(2,1)S(1)} %copy-done.3, bf16[512,4096]{1,0:T(8,128)(2,1)S(1)} %copy-done), custom_call_target="tpu_custom_call" | custom-call | tf_op jit(solution)/shard_map/pallas_call | solution.py:483
  77.0 0.8 %copy.6 = bf16[256,1024]{1,0:T(8,128)(2,1)} copy(bf16[256,1024]{1,0:T(8,128)(2,1)S(1)} %shard_map.46) | data formatting | bytes 1048576
Async XLA Ops:
  0.0 2.2 %copy-start = (bf16[512,4096]{1,0:T(8,128)(2,1)S(1)}, bf16[512,4096]{1,0:T(8,128)(2,1)}, u32[]{:S(2)}) copy-start(bf16[512,4096]{1,0:T(8,128)(2,1)} %w_ref.1) | copy-start | bytes 12582916
  2.2 0.9 %copy-start.1 = (bf16[256,512]{1,0:T(8,128)(2,1)S(1)}, bf16[256,512]{1,0:T(8,128)(2,1)}, u32[]{:S(2)}) copy-start(bf16[256,512]{1,0:T(8,128)(2,1)} %q_ref.1) | copy-start | bytes 786436
  3.1 0.8 %copy-start.2 = (bf16[256,128]{1,0:T(8,128)(2,1)S(1)}, bf16[256,128]{1,0:T(8,128)(2,1)}, u32[]{:S(2)}) copy-start(bf16[256,128]{1,0:T(8,128)(2,1)} %k_ref.1) | copy-start | bytes 196612
  4.0 0.8 %copy-start.3 = (bf16[256,128]{1,0:T(8,128)(2,1)S(1)}, bf16[256,128]{1,0:T(8,128)(2,1)}, u32[]{:S(2)}) copy-start(bf16[256,128]{1,0:T(8,128)(2,1)} %v_ref.1) | copy-start | bytes 196612

commit v2 on v1

v2 whole, which is shorter than its diff:
```python
import functools
import math

import jax
import jax.numpy as jnp
from jax import lax
from jax.experimental import pallas as pl
from jax.experimental.pallas import tpu as pltpu
from jax.sharding import PartitionSpec as P

HD = 128
ROWS = 256
NX, NZ = 4, 8
NU = 2 * NX
LOG2E = math.log2(math.e)
FLOOR = -1e30
PEN = 1e32
WCH = 4
MESH = pl.DeviceIdType.MESH
MIRROR = (0, 2, 1, 4, 3)
BF = jnp.bfloat16
F32 = jnp.float32


def low_of(x):
    return jnp.where(x == 0, 0, jnp.where(x == 1, 2, jnp.where(x == 2, 3, 1)))


def column_of(u):
    a = jnp.minimum(u, NU - 1 - u)
    return jnp.where(a == 0, 0, jnp.where(a == 1, 3, jnp.where(a == 2, 1, 2)))


def slot_of(u):
    return jnp.where(u < NX, 0, 1)


def dev(x, yl, z, yh, c):
    return {"ctx": (x * 2 + yl) * NZ + z, "head": yh * 2 + c}


def kernel(
    q_ref, k_ref, v_ref, w_ref, o_ref,
    vraw, vst, kvbuf, qbuf, s_ref, mx_ref, acc, m_ref, l_ref,
    osend, ssend, orecv, srecv, attsend, att, wbuf,
    sw_s, sw_r, qs_s, qs_r, z_s, z_r, sib_s, sib_r,
    w1_s, w1_r, w2_s, w2_r, w3_s, w3_r, wl, vl,
    os_s, os_r, at_s, at_r, as_s, as_r,
):
    ctx = lax.axis_index("ctx")
    head = lax.axis_index("head")
    x = ctx // (2 * NZ)
    yl = (ctx // NZ) % 2
    z = ctx % NZ
    yh = head // 2
    c = head % 2
    scale = LOG2E / math.sqrt(HD)
    D = functools.partial(dev)
    zp, zm = (z + 1) % NZ, (z + NZ - 1) % NZ

    vcopy = pltpu.make_async_copy(v_ref, vraw, vl)
    vcopy.start()
    barrier = pltpu.get_barrier_semaphore()
    partners = []
    for i in range(1, 4 * NX):
        partners.append(D((x + i // 4) % NX, (yl + (i // 2) % 2) % 2, z, yh, (c + i % 2) % 2))
    for i in range(4):
        partners.append(D(x if i < 2 else NX - 1 - x, i % 2, z, 1 - yh, c))
    partners.append(D(x, 1 - yl, z, 1 - yh, 1 - c))
    rel = [z, zm, zp, (z + NZ - 2) % NZ, (z + 2) % NZ, (z + NZ - 3) % NZ, (z + 3) % NZ,
           (z + NZ - 4) % NZ]
    partners += [D(x, yl, rel[r], yh, c) for r in (1, 2, 3, 4)]
    for p in partners:
        pl.semaphore_signal(barrier, inc=1, device_id=p, device_id_type=MESH)
    vcopy.wait()
    vst[0:HD, :] = vraw[0:HD, :].T
    vst[HD:ROWS, :] = vraw[HD:ROWS, :].T
    pl.semaphore_wait(barrier, len(partners))

    def rcopy(src, dst, ss, rs, to):
        return pltpu.make_async_remote_copy(
            src_ref=src, dst_ref=dst, send_sem=ss, recv_sem=rs, device_id=to, device_id_type=MESH
        )

    sib = D(x, yl, z, yh, 1 - c)
    lo = low_of(x)
    hi = NU - 1 - lo
    mine = 2 * x + yl

    col, slo = column_of(mine), slot_of(mine)
    home = D(col, c, z, yh, slo)
    stays = jnp.logical_and(jnp.logical_and(col == x, c == yl), slo == c)

    def kv_half(slot, zz, half):
        return kvbuf.at[slot, zz, pl.ds(half * ROWS, ROWS), :]

    kcp = rcopy(k_ref, kv_half(slo, z, 0), sw_s.at[0], sw_r.at[0], home)
    vcp = rcopy(vst, kv_half(slo, z, 1), sw_s.at[1], sw_r.at[1], home)
    klc = pltpu.make_async_copy(k_ref, kv_half(slo, z, 0), sw_r.at[0])
    vlc = pltpu.make_async_copy(vst, kv_half(slo, z, 1), sw_r.at[1])

    @pl.when(jnp.logical_not(stays))
    def _():
        kcp.start()
        vcp.start()

    @pl.when(stays)
    def _():
        klc.start()
        vlc.start()

    def q_src(d):
        return q_ref.at[:, pl.ds(d * 2 * HD, 2 * HD)]

    def q_each(remote, local):
        for i in range(NX):
            xt = (col + i) % NX
            for d in range(2):
                want = low_of(xt) <= mine
                here = jnp.logical_and(jnp.logical_and(xt == x, c == yl), c == d)

                @pl.when(jnp.logical_and(want, jnp.logical_not(here)))
                def _(i=i, d=d, xt=xt):
                    remote(rcopy(q_src(d), qbuf.at[mine], qs_s.at[i, d], qs_r.at[mine], D(xt, c, z, yh, d)))

                if local is not None:
                    @pl.when(jnp.logical_and(want, here))
                    def _(d=d):
                        local(pltpu.make_async_copy(q_src(d), qbuf.at[mine], qs_r.at[mine]))

    q_each(lambda cp: cp.start(), lambda cp: cp.start())

    DC = o_ref.shape[1]
    WR = w_ref.shape[0]
    WP = WR // WCH
    gw = yh * 2 + c
    xrow = (1 - yh) * 2 + yl
    yrow = (1 - yh) * 2 + (1 - yl)

    def w1(j, d):
        return rcopy(
            w_ref.at[pl.ds(j * WP, WP), pl.ds(((1 - yh) * 2 + d) * DC, DC)],
            wbuf.at[gw, pl.ds(j * WP, WP), :],
            w1_s.at[j, d], w1_r.at[j], D(x, 1 - yl, z, 1 - yh, d),
        )

    def w1_in(j):
        return rcopy(
            wbuf.at[xrow, pl.ds(j * WP, WP), :], wbuf.at[xrow, pl.ds(j * WP, WP), :],
            w2_s.at[j], w1_r.at[j], D(x, 1 - yl, z, yh, c),
        )

    def w2(j):
        return rcopy(
            wbuf.at[xrow, pl.ds(j * WP, WP), :], wbuf.at[xrow, pl.ds(j * WP, WP), :],
            w2_s.at[j], w2_r.at[j], D(x, 1 - yl, z, yh, c),
        )

    w3 = rcopy(
        w_ref.at[:, pl.ds((yh * 2 + 1 - c) * DC, DC)], wbuf.at[gw], w3_s, w3_r, sib
    )
    wown = pltpu.make_async_copy(w_ref.at[:, pl.ds(gw * DC, DC)], wbuf.at[gw], wl)

    def blk(slot, zz):
        return kvbuf.at[slot, zz]

    def zto(r):
        return D(x, yl, rel[r], yh, c)

    def own_to(r):
        return rcopy(blk(c, z), blk(c, z), z_s.at[r], z_r.at[MIRROR[r]], zto(r))

    def pass_on(r):
        return rcopy(blk(c, rel[r]), blk(c, rel[r]), z_s.at[r + 2], z_r.at[r + 2], zto(5 - r))

    def pass_half(r):
        h = r - 3
        return rcopy(half_of(c, rel[r], h), half_of(c, rel[r], h), z_s.at[r + 4], z_r.at[r + 4],
                     zto(7 - r))

    def tosib(r):
        return rcopy(blk(c, rel[r]), blk(c, rel[r]), sib_s.at[r], sib_r.at[r], sib)

    def half_of(slot, zz, h):
        return kvbuf.at[slot, zz, pl.ds(h * ROWS, ROWS), :]

    def arrive(r):
        if r == 7:
            for h in range(2):
                rcopy(half_of(c, rel[7], h), half_of(c, rel[7], h), z_s.at[0], z_r.at[7 + h], sib).wait_recv()
        else:
            rcopy(blk(c, rel[r]), blk(c, rel[r]), z_s.at[0], z_r.at[r], sib).wait_recv()
        if r in (3, 4):
            pass_on(r).start()
            pass_half(r).start()
        tosib(r).start()

    def sib_arrive(r):
        rcopy(blk(1 - c, rel[r]), blk(1 - c, rel[r]), sib_s.at[r], sib_r.at[r], sib).wait_recv()

    m_ref[...] = jnp.full_like(m_ref, FLOOR)
    l_ref[...] = jnp.zeros_like(l_ref)
    acc[...] = jnp.zeros_like(acc)

    for half in range(2):
        pltpu.make_async_copy(kv_half(c, z, half), kv_half(c, z, half), sw_r.at[half]).wait()
    for r in (3, 4, 1, 2):
        own_to(r).start()
    tosib(0).start()

    @pl.when(c != yl)
    def _():
        for j in range(WCH):
            for d in range(2):
                w1(j, d).start()

    def q_wait(u):
        pltpu.make_async_copy(qbuf.at[u], qbuf.at[u], qs_r.at[u]).wait()

    q_wait(lo)
    q_wait(hi)
    w3.start()
    wown.start()

    def hs(h):
        return slice(h * ROWS, (h + 1) * ROWS)

    def qk(slot, zz, u, h):
        return lax.dot_general(
            kvbuf[slot, zz, 0:ROWS, :], qbuf[u, :, h * HD:(h + 1) * HD],
            (((1,), (1,)), ((), ())), preferred_element_type=F32,
        )

    def vt(slot, zz):
        return jnp.concatenate(
            [kvbuf[slot, zz, ROWS:ROWS + HD, :], kvbuf[slot, zz, ROWS + HD:2 * ROWS, :]], axis=1
        )

    def pv(slot, zz, p):
        return lax.dot_general(
            vt(slot, zz), p.astype(BF), (((1,), (0,)), ((), ())), preferred_element_type=F32
        )

    def fold(a, op):
        return op(a.reshape(a.shape[0] // 8, 8, a.shape[1]), axis=0)

    def diagonal(slot, u):
        key_i = lax.broadcasted_iota(jnp.int32, (ROWS, ROWS), 0)
        qry_i = lax.broadcasted_iota(jnp.int32, (ROWS, ROWS), 1)
        allowed = key_i <= qry_i
        for h in range(2):
            s = jnp.where(allowed, qk(slot, z, u, h) * scale, -PEN)
            m = jnp.max(s, axis=0, keepdims=True)
            p = jnp.exp2(s - m)
            m_ref[u, 0:1, hs(h)] = m
            l_ref[u, :, hs(h)] = fold(p, jnp.sum)
            acc[u, :, hs(h)] = pv(slot, z, p)

    def chunk(slot):
        return jnp.where(slot == 0, lo, hi)

    def pen(slot, zz, u):
        kid = chunk(slot) * NZ + zz
        return jnp.where(kid < u * NZ + z, 0.0, PEN).astype(F32)

    def score(blocks, u, h):
        mx = None
        for b, (slot, zz) in enumerate(blocks):
            s = qk(slot, zz, u, h)
            s_ref[b * ROWS:(b + 1) * ROWS, hs(h)] = s
            top = fold(s, jnp.max) - pen(slot, zz, u)
            mx = top if mx is None else jnp.maximum(mx, top)
        mx_ref[:, hs(h)] = mx

    def absorb(blocks, u, blocks_next, un, h):
        m_old = m_ref[u, 0:1, hs(h)]
        m_new = jnp.maximum(m_old, jnp.max(mx_ref[:, hs(h)], axis=0, keepdims=True) * scale)
        alpha = jnp.exp2(m_old - m_new)
        m_ref[u, 0:1, hs(h)] = m_new
        l8, out = None, None
        for b, (slot, zz) in enumerate(blocks):
            p = jnp.exp2(s_ref[b * ROWS:(b + 1) * ROWS, hs(h)] * scale - (m_new + pen(slot, zz, u)))
            p8 = fold(p, jnp.sum)
            l8 = p8 if l8 is None else l8 + p8
            d = pv(slot, zz, p)
            out = d if out is None else out + d
        score(blocks_next, un, h)
        l_ref[u, :, hs(h)] = l_ref[u, :, hs(h)] * alpha + l8
        acc[u, :, hs(h)] = acc[u, :, hs(h)] * alpha + out

    diagonal(c, chunk(c))
    sib_arrive(0)
    diagonal(1 - c, chunk(1 - c))

    def o_send(u):
        return rcopy(osend.at[u], orecv.at[x, slot_of(u)], os_s.at[u, 0],
                     os_r.at[x, slot_of(u), 0], D(column_of(u), yl, z, yh, c))

    def st_send(u):
        return rcopy(ssend.at[u], srecv.at[x, slot_of(u)], os_s.at[u, 1],
                     os_r.at[x, slot_of(u), 1], D(column_of(u), yl, z, yh, c))

    def w_on(j):
        w1_in(j).wait_recv()
        w2(j).start()

    for r in (3, 4, 1):
        arrive(r)
    for r in (3, 4, 1):
        sib_arrive(r)
    NU1 = NU + 1

    def unit(i):
        j = jnp.where(i < NU1, NU - i, i - NU1)
        u = jnp.where(j < 2 * lo, NU - 1 - j // 2, jnp.where(j < NU - 2, NU - 2 - j + lo, jnp.where(
            j < NU, hi, lo)))
        slot = jnp.where(j < 2 * lo, 1 - j % 2, jnp.where(j == NU - 2, 1, 0))
        zs = [jnp.where(i < NU1, rel[r0], rel[r1]) for r0, r1 in ((0, 2), (3, 5), (4, 6), (1, 7))]
        return u, slot, [(slot, zz) for zz in zs]

    def begin(_):
        u, _, blocks = unit(jnp.int32(0))
        for h in range(2):
            score(blocks, u, h)

    begin(0)

    def one(i, _):
        u, slot, blocks = unit(i)
        un, _, blocks_n = unit(jnp.minimum(i + 1, 2 * NU1 - 1))

        @pl.when(i == 3)
        def _():
            arrive(2)

        @pl.when(i == 6)
        def _():
            for r in (5, 6, 7):
                arrive(r)

        @pl.when(i == 8)
        def _():
            for r in (2, 5, 6, 7):
                sib_arrive(r)
            w_on(0)

        for k, at in ((1, 12), (2, 15)):
            @pl.when(i == at)
            def _():
                w_on(k)

        @pl.when(jnp.logical_and(jnp.logical_and(i < NU, un != u), jnp.logical_and(un != lo, un != hi)))
        def _():
            q_wait(un)

        for h in range(2):
            absorb(blocks, u, blocks_n, un, h)

        @pl.when(jnp.logical_and(jnp.logical_and(i >= NU1, slot == 0), jnp.logical_and(u != lo, u != hi)))
        def _():
            osend[u] = acc[u].astype(BF)
            lsum = jnp.sum(l_ref[u], axis=0, keepdims=True)
            ssend[u] = jnp.concatenate(
                [jnp.broadcast_to(m_ref[u, 0:1, :], (4, 2 * ROWS)),
                 jnp.broadcast_to(lsum, (4, 2 * ROWS))], axis=0)
            o_send(u).start()
            st_send(u).start()

        return 0

    lax.fori_loop(0, 2 * NU1, one, 0)
    w_on(3)

    g = yh * 2 + yl

    def chunk_of(s):
        return lo if s == 0 else hi

    def owner(s, t):
        u = chunk_of(s)
        return D(u // 2, u % 2, z, t, c)

    def owned(s, t):
        u = chunk_of(s)
        return jnp.logical_and(u == mine, yh == t)

    def a_remote(s, t):
        return rcopy(attsend.at[s], att.at[g, c], at_s.at[s, t], at_r.at[g], owner(s, t))

    def a_local(s):
        return pltpu.make_async_copy(attsend.at[s], att.at[g, c], at_r.at[g])

    for s in (1, 0):
        u = chunk_of(s)
        l_ref[u, 0:1, :] = jnp.sum(l_ref[u], axis=0, keepdims=True)

        def merge(xs, s=s, u=u):
            rcopy(osend.at[u], orecv.at[xs, s], os_s.at[u, 0], os_r.at[xs, s, 0], sib).wait_recv()
            rcopy(ssend.at[u], srecv.at[xs, s], os_s.at[u, 1], os_r.at[xs, s, 1], sib).wait_recv()
            m_old = m_ref[u, 0:1, :]
            m_in = srecv[xs, s, 0:1, :]
            m_new = jnp.maximum(m_old, m_in)
            a_old = jnp.exp2(m_old - m_new)
            a_in = jnp.exp2(m_in - m_new)
            m_ref[u, 0:1, :] = m_new
            l_ref[u, 0:1, :] = l_ref[u, 0:1, :] * a_old + srecv[xs, s, 4:5, :] * a_in
            acc[u] = acc[u] * a_old + orecv[xs, s].astype(F32) * a_in

        for xs in range(NX):
            pl.when(jnp.logical_and(xs != x, low_of(xs) <= u))(functools.partial(merge, xs))
        for h in range(2):
            o = acc[u, :, hs(h)] / l_ref[u, 0:1, hs(h)]
            attsend[s, :, h * HD:(h + 1) * HD] = o.T.astype(BF)
        for t in range(2):
            here = owned(s, t)

            @pl.when(here)
            def _():
                a_local(s).start()

            @pl.when(jnp.logical_not(here))
            def _():
                a_remote(s, t).start()

    def a_sib(gg):
        return rcopy(att.at[gg, c], att.at[gg, c], as_s.at[gg], as_r.at[gg], sib)

    for gg in range(4):
        pltpu.make_async_copy(attsend.at[0], att.at[gg, c], at_r.at[gg]).wait()
        a_sib(gg).start()
    w3.wait_recv()
    wown.wait()
    for j in range(WCH):
        rcopy(wbuf.at[yrow, pl.ds(j * WP, WP), :], wbuf.at[yrow, pl.ds(j * WP, WP), :],
              w2_s.at[j], w2_r.at[j], sib).wait_recv()
    for gg in range(4):
        rcopy(att.at[gg, 1 - c], att.at[gg, 1 - c], as_s.at[gg], as_r.at[gg], sib).wait_recv()

    rows = jnp.concatenate([att[i // 2, i % 2] for i in range(8)], axis=1)
    for j in range(DC // 256):
        cs = slice(j * 256, (j + 1) * 256)
        wcol = jnp.concatenate([wbuf[i, :, cs] for i in range(4)], axis=0)
        o_ref[:, cs] = jnp.dot(rows, wcol, preferred_element_type=F32).astype(BF)

    @pl.when(jnp.logical_not(stays))
    def _():
        kcp.wait_send()
        vcp.wait_send()

    q_each(lambda cp: cp.wait_send(), None)

    @pl.when(c != yl)
    def _():
        for j in range(WCH):
            for d in range(2):
                w1(j, d).wait_send()
    for j in range(WCH):
        w2(j).wait_send()
    w3.wait_send()
    for r in (1, 2, 3, 4):
        own_to(r).wait_send()
    for r in (3, 4):
        pass_on(r).wait_send()
        pass_half(r).wait_send()
    for r in range(8):
        tosib(r).wait_send()

    def sent(u, _):
        @pl.when(jnp.logical_and(u != lo, u != hi))
        def _():
            o_send(u).wait_send()
            st_send(u).wait_send()

        return 0

    lax.fori_loop(lo, NU, sent, 0)
    for s in range(2):
        for t in range(2):
            @pl.when(jnp.logical_not(owned(s, t)))
            def _():
                a_remote(s, t).wait_send()
    for gg in range(4):
        a_sib(gg).wait_send()


def per_device(query, keys, values, out_weight):
    rows = query.shape[0]
    d_model = out_weight.shape[1]
    dma = pltpu.SemaphoreType.DMA
    vm = pl.BlockSpec(memory_space=pltpu.VMEM)
    hbm = pl.BlockSpec(memory_space=pltpu.HBM)
    R2 = 2 * ROWS
    return pl.pallas_call(
        kernel,
        out_shape=jax.ShapeDtypeStruct((rows, d_model // 4), BF),
        in_specs=[hbm, hbm, hbm, hbm],
        out_specs=vm,
        scratch_shapes=[
            pltpu.VMEM((ROWS, HD), BF),
            pltpu.VMEM((ROWS, HD), BF),
            pltpu.VMEM((2, NZ, R2, HD), BF),
            pltpu.VMEM((NU, ROWS, 2 * HD), BF),
            pltpu.VMEM((4 * ROWS, R2), F32),
            pltpu.VMEM((8, R2), F32),
            pltpu.VMEM((NU, HD, R2), F32),
            pltpu.VMEM((NU, 8, R2), F32),
            pltpu.VMEM((NU, 8, R2), F32),
            pltpu.VMEM((NU, HD, R2), BF),
            pltpu.VMEM((NU, 8, R2), F32),
            pltpu.VMEM((NX, 2, HD, R2), BF),
            pltpu.VMEM((NX, 2, 8, R2), F32),
            pltpu.VMEM((2, ROWS, 2 * HD), BF),
            pltpu.VMEM((4, 2, ROWS, 2 * HD), BF),
            pltpu.VMEM((4, out_weight.shape[0], d_model // 4), BF),
            dma((2,)), dma((2,)),
            dma((NX, 2)), dma((NU,)),
            dma((9,)), dma((9,)),
            dma((8,)), dma((8,)),
            dma((WCH, 2)), dma((WCH,)), dma((WCH,)), dma((WCH,)), dma, dma, dma, dma,
            dma((NU, 2)), dma((NX, 2, 2)),
            dma((2, 2)), dma((4,)), dma((4,)), dma((4,)),
        ],
        compiler_params=pltpu.CompilerParams(
            collective_id=0, has_side_effects=True, vmem_limit_bytes=48 * 1024 * 1024
        ),
    )(query, keys, values, out_weight)


def solution(mesh):
    return jax.shard_map(
        per_device,
        mesh=mesh,
        in_specs=(P("ctx", "head"), P("ctx", "head"), P("ctx", "head"), P("head", None)),
        out_specs=P("ctx", "head"),
        check_vma=False,
    )
```

time: 78.6 us -> 77.3 us (0.983)
  the two profiles are of different devices: /device:TPU:3 before, /device:TPU:1 now
where the time goes in v2:
time: 77.3 us; the launch traced here: 77 us
  Pallas kernels  71.4 us (92%)
  local copies, waits for them, and re-layouts  5.61 us (7%)
    pallas_call x1, Pallas kernels, per_device(): pl.pallas_call(kernel, out_shape=jax.ShapeDtypeStruct((rows, d_model // 4...  71.4 us
    unnamed x9, local copies, waits for them, and re-layouts  5.61 us

profile of v2, /device:TPU:1, one launch (start us, length us, event | category | flops | bytes accessed | tf_op | source)
XLA Modules:
  0.0 77.0 jit_solution(18149961426559804717)
XLA Ops:
  0.0 0.0 copy-start
  0.0 2.2 %copy-done = bf16[512,4096]{1,0:T(8,128)(2,1)S(1)} copy-done((bf16[512,4096]{1,0:T(8,128)(2,1)S(1)}, bf16[512,4096]{1,0:T(8,128)(2,1)}, u32[]{:S(2)}) %copy-start) | copy-done | bytes 4194328
  2.2 0.0 copy-start.1
  2.2 0.9 %copy-done.1 = bf16[256,512]{1,0:T(8,128)(2,1)S(1)} copy-done((bf16[256,512]{1,0:T(8,128)(2,1)S(1)}, bf16[256,512]{1,0:T(8,128)(2,1)}, u32[]{:S(2)}) %copy-start.1) | copy-done | bytes 262168
  3.1 0.0 copy-start.2
  3.1 0.8 %copy-done.2 = bf16[256,128]{1,0:T(8,128)(2,1)S(1)} copy-done((bf16[256,128]{1,0:T(8,128)(2,1)S(1)}, bf16[256,128]{1,0:T(8,128)(2,1)}, u32[]{:S(2)}) %copy-start.2) | copy-done | bytes 65560
  4.0 0.0 copy-start.3
  4.0 0.8 %copy-done.3 = bf16[256,128]{1,0:T(8,128)(2,1)S(1)} copy-done((bf16[256,128]{1,0:T(8,128)(2,1)S(1)}, bf16[256,128]{1,0:T(8,128)(2,1)}, u32[]{:S(2)}) %copy-start.3) | copy-done | bytes 65560
  4.8 71.4 %shard_map.46 = bf16[256,1024]{1,0:T(8,128)(2,1)S(1)} custom-call(bf16[256,512]{1,0:T(8,128)(2,1)S(1)} %copy-done.1, bf16[256,128]{1,0:T(8,128)(2,1)S(1)} %copy-done.2, bf16[256,128]{1,0:T(8,128)(2,1)S(1)} %copy-done.3, bf16[512,4096]{1,0:T(8,128)(2,1)S(1)} %copy-done), custom_call_target="tpu_custom_call" | custom-call | tf_op jit(solution)/shard_map/pallas_call | solution.py:493
  76.2 0.8 %copy.6 = bf16[256,1024]{1,0:T(8,128)(2,1)} copy(bf16[256,1024]{1,0:T(8,128)(2,1)S(1)} %shard_map.46) | data formatting | bytes 1048576
Async XLA Ops:
  0.0 2.2 %copy-start = (bf16[512,4096]{1,0:T(8,128)(2,1)S(1)}, bf16[512,4096]{1,0:T(8,128)(2,1)}, u32[]{:S(2)}) copy-start(bf16[512,4096]{1,0:T(8,128)(2,1)} %w_ref.1) | copy-start | bytes 12582916
  2.2 0.9 %copy-start.1 = (bf16[256,512]{1,0:T(8,128)(2,1)S(1)}, bf16[256,512]{1,0:T(8,128)(2,1)}, u32[]{:S(2)}) copy-start(bf16[256,512]{1,0:T(8,128)(2,1)} %q_ref.1) | copy-start | bytes 786436
  3.1 0.8 %copy-start.2 = (bf16[256,128]{1,0:T(8,128)(2,1)S(1)}, bf16[256,128]{1,0:T(8,128)(2,1)}, u32[]{:S(2)}) copy-start(bf16[256,128]{1,0:T(8,128)(2,1)} %k_ref.1) | copy-start | bytes 196612
  4.0 0.8 %copy-start.3 = (bf16[256,128]{1,0:T(8,128)(2,1)S(1)}, bf16[256,128]{1,0:T(8,128)(2,1)}, u32[]{:S(2)}) copy-start(bf16[256,128]{1,0:T(8,128)(2,1)} %v_ref.1) | copy-start | bytes 196612

commit v3 on v2

--- a/solution.py
+++ b/solution.py
@@ -23,16 +23,15 @@
 
 
 def low_of(x):
-    return jnp.where(x == 0, 0, jnp.where(x == 1, 2, jnp.where(x == 2, 3, 1)))
+    return 2 * x
 
 
 def column_of(u):
-    a = jnp.minimum(u, NU - 1 - u)
-    return jnp.where(a == 0, 0, jnp.where(a == 1, 3, jnp.where(a == 2, 1, 2)))
+    return u // 2
 
 
 def slot_of(u):
-    return jnp.where(u < NX, 0, 1)
+    return u % 2
 
 
 def dev(x, yl, z, yh, c):
@@ -64,8 +63,8 @@
     partners = []
     for i in range(1, 4 * NX):
         partners.append(D((x + i // 4) % NX, (yl + (i // 2) % 2) % 2, z, yh, (c + i % 2) % 2))
-    for i in range(4):
-        partners.append(D(x if i < 2 else NX - 1 - x, i % 2, z, 1 - yh, c))
+    for i in range(2):
+        partners.append(D(x, i, z, 1 - yh, c))
     partners.append(D(x, 1 - yl, z, 1 - yh, 1 - c))
     rel = [z, zm, zp, (z + NZ - 2) % NZ, (z + 2) % NZ, (z + NZ - 3) % NZ, (z + 3) % NZ,
            (z + NZ - 4) % NZ]
@@ -84,7 +83,9 @@
 
     sib = D(x, yl, z, yh, 1 - c)
     lo = low_of(x)
-    hi = NU - 1 - lo
+    hi = lo + 1
+    top = jnp.where(x == 0, NU - 3, NU - 1)
+    at_end = x == NX - 1
     mine = 2 * x + yl
 
     col, slo = column_of(mine), slot_of(mine)
@@ -99,10 +100,19 @@
     klc = pltpu.make_async_copy(k_ref, kv_half(slo, z, 0), sw_r.at[0])
     vlc = pltpu.make_async_copy(vst, kv_half(slo, z, 1), sw_r.at[1])
 
+    home2 = D(NX - 1, c, z, yh, slo)
+    kcp2 = rcopy(k_ref, kv_half(2 + slo, z, 0), sw_s.at[2], sw_r.at[2], home2)
+    vcp2 = rcopy(vst, kv_half(2 + slo, z, 1), sw_s.at[3], sw_r.at[3], home2)
+
     @pl.when(jnp.logical_not(stays))
     def _():
         kcp.start()
         vcp.start()
+
+    @pl.when(x == 0)
+    def _():
+        kcp2.start()
+        vcp2.start()
 
     @pl.when(stays)
     def _():
@@ -116,7 +126,7 @@
         for i in range(NX):
             xt = (col + i) % NX
             for d in range(2):
-                want = low_of(xt) <= mine
+                want = jnp.logical_and(low_of(xt) <= mine, jnp.logical_or(xt > 0, mine < NU - 2))
                 here = jnp.logical_and(jnp.logical_and(xt == x, c == yl), c == d)
 
                 @pl.when(jnp.logical_and(want, jnp.logical_not(here)))
@@ -128,7 +138,6 @@
                     def _(d=d):
                         local(pltpu.make_async_copy(q_src(d), qbuf.at[mine], qs_r.at[mine]))
 
-    q_each(lambda cp: cp.start(), lambda cp: cp.start())
 
     DC = o_ref.shape[1]
     WR = w_ref.shape[0]
@@ -167,52 +176,86 @@
     def zto(r):
         return D(x, yl, rel[r], yh, c)
 
-    def own_to(r):
-        return rcopy(blk(c, z), blk(c, z), z_s.at[r], z_r.at[MIRROR[r]], zto(r))
-
-    def pass_on(r):
-        return rcopy(blk(c, rel[r]), blk(c, rel[r]), z_s.at[r + 2], z_r.at[r + 2], zto(5 - r))
-
-    def pass_half(r):
-        h = r - 3
-        return rcopy(half_of(c, rel[r], h), half_of(c, rel[r], h), z_s.at[r + 4], z_r.at[r + 4],
-                     zto(7 - r))
-
-    def tosib(r):
-        return rcopy(blk(c, rel[r]), blk(c, rel[r]), sib_s.at[r], sib_r.at[r], sib)
-
     def half_of(slot, zz, h):
         return kvbuf.at[slot, zz, pl.ds(h * ROWS, ROWS), :]
 
-    def arrive(r):
-        if r == 7:
-            for h in range(2):
-                rcopy(half_of(c, rel[7], h), half_of(c, rel[7], h), z_s.at[0], z_r.at[7 + h], sib).wait_recv()
-        else:
-            rcopy(blk(c, rel[r]), blk(c, rel[r]), z_s.at[0], z_r.at[r], sib).wait_recv()
-        if r in (3, 4):
-            pass_on(r).start()
-            pass_half(r).start()
-        tosib(r).start()
-
-    def sib_arrive(r):
-        rcopy(blk(1 - c, rel[r]), blk(1 - c, rel[r]), sib_s.at[r], sib_r.at[r], sib).wait_recv()
-
+    def own_to(r, h, e=0):
+        src = half_of(2 * e + c, z, h)
+        return rcopy(src, src, z_s.at[e, r, h], z_r.at[e, MIRROR[r], h], zto(r))
+
+    def pass_on(r, h, e=0):
+        src = half_of(2 * e + c, rel[r], h)
+        return rcopy(src, src, z_s.at[e, r + 2, h], z_r.at[e, r + 2, h], zto(5 - r))
+
+    def pass_half(r, e=0):
+        src = half_of(2 * e + c, rel[r], r - 3)
+        return rcopy(src, src, z_s.at[e, 7, r - 3], z_r.at[e, 7, r - 3], zto(7 - r))
+
+    def tosib(r, e=0):
+        src = blk(2 * e + c, rel[r])
+        return rcopy(src, src, sib_s.at[e, r], sib_r.at[e, r], sib)
+
+    def landed(r, h, e):
+        src = half_of(2 * e + c, rel[r], h)
+        rcopy(src, src, z_s.at[e, 0, 0], z_r.at[e, r, h], sib).wait_recv()
+
+    def arrive(r, e=0):
+        for h in range(2):
+            landed(r, h, e)
+        tosib(r, e).start()
+
+    def arrive_two(e=0):
+        for h in range(2):
+            for r in (3, 4):
+                landed(r, h, e)
+                pass_on(r, h, e).start()
+                if h == r - 3:
+                    pass_half(r, e).start()
+        for r in (3, 4):
+            tosib(r, e).start()
+
+    def sib_arrive(r, e=0):
+        src = blk(2 * e + 1 - c, rel[r])
+        rcopy(src, src, sib_s.at[e, r], sib_r.at[e, r], sib).wait_recv()
+
+    def launch_two(e):
+        for h in range(2):
+            src = half_of(2 * e + c, z, h)
+            pltpu.make_async_copy(src, src, sw_r.at[2 * e + h]).wait()
+            for r in (3, 4):
+                own_to(r, h, e).start()
+        tosib(0, e).start()
+
+    def launch_one(e):
+        for h in range(2):
+            for r in (3, 4):
+                own_to(r, h, e).wait_send()
+            for r in (1, 2):
+                own_to(r, h, e).start()
+
+    def drained(e):
+        for h in range(2):
+            for r in (1, 2):
+                own_to(r, h, e).wait_send()
+            for r in (3, 4):
+                pass_on(r, h, e).wait_send()
+        for r in (3, 4):
+            pass_half(r, e).wait_send()
+        for r in range(8):
+            tosib(r, e).wait_send()
+
+    @pl.when(c != yl)
+    def _():
+        for j in range(WCH):
+            for d in range(2):
+                w1(j, d).start()
+
+    q_each(lambda cp: cp.start(), lambda cp: cp.start())
     m_ref[...] = jnp.full_like(m_ref, FLOOR)
     l_ref[...] = jnp.zeros_like(l_ref)
     acc[...] = jnp.zeros_like(acc)
 
-    for half in range(2):
-        pltpu.make_async_copy(kv_half(c, z, half), kv_half(c, z, half), sw_r.at[half]).wait()
-    for r in (3, 4, 1, 2):
-        own_to(r).start()
-    tosib(0).start()
-
-    @pl.when(c != yl)
-    def _():
-        for j in range(WCH):
-            for d in range(2):
-                w1(j, d).start()
+    launch_two(0)
 
     def q_wait(u):
         pltpu.make_async_copy(qbuf.at[u], qbuf.at[u], qs_r.at[u]).wait()
@@ -257,7 +300,7 @@
             acc[u, :, hs(h)] = pv(slot, z, p)
 
     def chunk(slot):
-        return jnp.where(slot == 0, lo, hi)
+        return jnp.where(slot < 2, lo + slot, slot - 2)
 
     def pen(slot, zz, u):
         kid = chunk(slot) * NZ + zz
@@ -289,8 +332,13 @@
         acc[u, :, hs(h)] = acc[u, :, hs(h)] * alpha + out
 
     diagonal(c, chunk(c))
+    launch_one(0)
     sib_arrive(0)
     diagonal(1 - c, chunk(1 - c))
+
+    @pl.when(at_end)
+    def _():
+        launch_two(1)
 
     def o_send(u):
         return rcopy(osend.at[u], orecv.at[x, slot_of(u)], os_s.at[u, 0],
@@ -300,77 +348,6 @@
         return rcopy(ssend.at[u], srecv.at[x, slot_of(u)], os_s.at[u, 1],
                      os_r.at[x, slot_of(u), 1], D(column_of(u), yl, z, yh, c))
 
-    def w_on(j):
-        w1_in(j).wait_recv()
-        w2(j).start()
-
-    for r in (3, 4, 1):
-        arrive(r)
-    for r in (3, 4, 1):
-        sib_arrive(r)
-    NU1 = NU + 1
-
-    def unit(i):
-        j = jnp.where(i < NU1, NU - i, i - NU1)
-        u = jnp.where(j < 2 * lo, NU - 1 - j // 2, jnp.where(j < NU - 2, NU - 2 - j + lo, jnp.where(
-            j < NU, hi, lo)))
-        slot = jnp.where(j < 2 * lo, 1 - j % 2, jnp.where(j == NU - 2, 1, 0))
-        zs = [jnp.where(i < NU1, rel[r0], rel[r1]) for r0, r1 in ((0, 2), (3, 5), (4, 6), (1, 7))]
-        return u, slot, [(slot, zz) for zz in zs]
-
-    def begin(_):
-        u, _, blocks = unit(jnp.int32(0))
-        for h in range(2):
-            score(blocks, u, h)
-
-    begin(0)
-
-    def one(i, _):
-        u, slot, blocks = unit(i)
-        un, _, blocks_n = unit(jnp.minimum(i + 1, 2 * NU1 - 1))
-
-        @pl.when(i == 3)
-        def _():
-            arrive(2)
-
-        @pl.when(i == 6)
-        def _():
-            for r in (5, 6, 7):
-                arrive(r)
-
-        @pl.when(i == 8)
-        def _():
-            for r in (2, 5, 6, 7):
-                sib_arrive(r)
-            w_on(0)
-
-        for k, at in ((1, 12), (2, 15)):
-            @pl.when(i == at)
-            def _():
-                w_on(k)
-
-        @pl.when(jnp.logical_and(jnp.logical_and(i < NU, un != u), jnp.logical_and(un != lo, un != hi)))
-        def _():
-            q_wait(un)
-
-        for h in range(2):
-            absorb(blocks, u, blocks_n, un, h)
-
-        @pl.when(jnp.logical_and(jnp.logical_and(i >= NU1, slot == 0), jnp.logical_and(u != lo, u != hi)))
-        def _():
-            osend[u] = acc[u].astype(BF)
-            lsum = jnp.sum(l_ref[u], axis=0, keepdims=True)
-            ssend[u] = jnp.concatenate(
-                [jnp.broadcast_to(m_ref[u, 0:1, :], (4, 2 * ROWS)),
-                 jnp.broadcast_to(lsum, (4, 2 * ROWS))], axis=0)
-            o_send(u).start()
-            st_send(u).start()
-
-        return 0
-
-    lax.fori_loop(0, 2 * NU1, one, 0)
-    w_on(3)
-
     g = yh * 2 + yl
 
     def chunk_of(s):
@@ -390,7 +367,7 @@
     def a_local(s):
         return pltpu.make_async_copy(attsend.at[s], att.at[g, c], at_r.at[g])
 
-    for s in (1, 0):
+    def finish(s):
         u = chunk_of(s)
         l_ref[u, 0:1, :] = jnp.sum(l_ref[u], axis=0, keepdims=True)
 
@@ -407,7 +384,8 @@
             acc[u] = acc[u] * a_old + orecv[xs, s].astype(F32) * a_in
 
         for xs in range(NX):
-            pl.when(jnp.logical_and(xs != x, low_of(xs) <= u))(functools.partial(merge, xs))
+            there = xs < x if xs > 0 else jnp.logical_and(x > 0, x < NX - 1)
+            pl.when(there)(functools.partial(merge, xs))
         for h in range(2):
             o = acc[u, :, hs(h)] / l_ref[u, 0:1, hs(h)]
             attsend[s, :, h * HD:(h + 1) * HD] = o.T.astype(BF)
@@ -421,6 +399,122 @@
             @pl.when(jnp.logical_not(here))
             def _():
                 a_remote(s, t).start()
+
+    def w_on(j):
+        w1_in(j).wait_recv()
+        w2(j).start()
+
+    def events(seg):
+        if seg == 0:
+            arrive_two()
+            w_on(0)
+            sib_arrive(3)
+        if seg == 1:
+            arrive(1)
+            arrive(2)
+            pl.when(at_end)(functools.partial(launch_one, 1))
+            w_on(1)
+        if seg == 2:
+            sib_arrive(1)
+            sib_arrive(4)
+
+            @pl.when(at_end)
+            def _():
+                arrive_two(1)
+
+            w_on(2)
+        if seg == 3:
+            arrive(5)
+            arrive(6)
+            arrive(7)
+        if seg == 4:
+            for r in (2, 5, 6, 7):
+                sib_arrive(r)
+            w_on(3)
+        if seg == 6:
+            @pl.when(at_end)
+            def _():
+                for r in (1, 2, 5, 6, 7):
+                    arrive(r, 1)
+                for r in range(8):
+                    sib_arrive(r, 1)
+
+    groups = ((0, 3), (1, 4), (2, 5), (6, 7))
+
+    def zpick(k, r0):
+        return jnp.where(k == 0, rel[r0[0]], jnp.where(k == 1, rel[r0[1]], jnp.where(
+            k == 2, rel[r0[2]], rel[r0[3]])))
+
+    def group(k, base):
+        za = zpick(k, [gr[0] for gr in groups])
+        zb = zpick(k, [gr[1] for gr in groups])
+        return [(base, za), (base + 1, za), (base, zb), (base + 1, zb)]
+
+    n = top - lo + 1
+    far = top - hi
+
+    def pick(seg, *values):
+        out = values[-1]
+        for e in range(len(values) - 2, -1, -1):
+            out = jnp.where(seg == e, values[e], out)
+        return out
+
+    def segment(seg, _):
+        for e in (0, 1, 2, 3, 4, 6):
+            pl.when(seg == e)(functools.partial(events, e))
+        first = pick(seg, 0, n // 2, 0, far // 2, 0, 0, 0)
+        end = pick(seg, n // 2, n, far // 2, far, 2 * far, 6, jnp.where(at_end, 8, 0))
+        count = pick(seg, n, n, far, far, 2 * far, 6, 8)
+        base = jnp.where(seg == 6, 2, 0)
+
+        def at(i):
+            return pick(seg, lo + i, lo + i, hi + 1 + i, hi + 1 + i, top - i // 2,
+                        hi - i // 3, hi - i // 4)
+
+        def grp(i):
+            return group(pick(seg, 0, 0, 1, 1, 2 + i % 2, 1 + i % 3, i % 4), base)
+
+        @pl.when(jnp.logical_and(first == 0, end > 0))
+        def _():
+            for h in range(2):
+                score(grp(0), at(0), h)
+
+        def one(i, _):
+            u = at(i)
+            nxt = jnp.minimum(i + 1, count - 1)
+            un = at(nxt)
+
+            @pl.when(jnp.logical_and(seg < 2, jnp.logical_and(un > u, un > hi)))
+            def _():
+                q_wait(un)
+
+            for h in range(2):
+                absorb(grp(i), u, grp(nxt), un, h)
+
+            @pl.when(jnp.logical_and(seg == 4, i % 2 == 1))
+            def _():
+                osend[u] = acc[u].astype(BF)
+                lsum = jnp.sum(l_ref[u], axis=0, keepdims=True)
+                ssend[u] = jnp.concatenate(
+                    [jnp.broadcast_to(m_ref[u, 0:1, :], (4, 2 * ROWS)),
+                     jnp.broadcast_to(lsum, (4, 2 * ROWS))], axis=0)
+                o_send(u).start()
+                st_send(u).start()
+
+            complete = jnp.where(at_end, jnp.logical_and(seg == 6, i == 3),
+                                 jnp.logical_and(seg == 5, i == 2))
+
+            @pl.when(complete)
+            def _():
+                finish(1)
+
+            return 0
+
+        lax.fori_loop(first, end, one, 0)
+        return 0
+
+    lax.fori_loop(0, 7, segment, 0)
+    finish(0)
 
     def a_sib(gg):
         return rcopy(att.at[gg, c], att.at[gg, c], as_s.at[gg], as_r.at[gg], sib)
@@ -447,6 +541,11 @@
         kcp.wait_send()
         vcp.wait_send()
 
+    @pl.when(x == 0)
+    def _():
+        kcp2.wait_send()
+        vcp2.wait_send()
+
     q_each(lambda cp: cp.wait_send(), None)
 
     @pl.when(c != yl)
@@ -457,23 +556,18 @@
     for j in range(WCH):
         w2(j).wait_send()
     w3.wait_send()
-    for r in (1, 2, 3, 4):
-        own_to(r).wait_send()
-    for r in (3, 4):
-        pass_on(r).wait_send()
-        pass_half(r).wait_send()
-    for r in range(8):
-        tosib(r).wait_send()
+    drained(0)
+
+    @pl.when(at_end)
+    def _():
+        drained(1)
 
     def sent(u, _):
-        @pl.when(jnp.logical_and(u != lo, u != hi))
-        def _():
-            o_send(u).wait_send()
-            st_send(u).wait_send()
-
+        o_send(u).wait_send()
+        st_send(u).wait_send()
         return 0
 
-    lax.fori_loop(lo, NU, sent, 0)
+    lax.fori_loop(hi + 1, top + 1, sent, 0)
     for s in range(2):
         for t in range(2):
             @pl.when(jnp.logical_not(owned(s, t)))
@@ -498,7 +592,7 @@
         scratch_shapes=[
             pltpu.VMEM((ROWS, HD), BF),
             pltpu.VMEM((ROWS, HD), BF),
-            pltpu.VMEM((2, NZ, R2, HD), BF),
+            pltpu.VMEM((4, NZ, R2, HD), BF),
             pltpu.VMEM((NU, ROWS, 2 * HD), BF),
             pltpu.VMEM((4 * ROWS, R2), F32),
             pltpu.VMEM((8, R2), F32),
@@ -512,10 +606,10 @@
             pltpu.VMEM((2, ROWS, 2 * HD), BF),
             pltpu.VMEM((4, 2, ROWS, 2 * HD), BF),
             pltpu.VMEM((4, out_weight.shape[0], d_model // 4), BF),
-            dma((2,)), dma((2,)),
+            dma((4,)), dma((4,)),
             dma((NX, 2)), dma((NU,)),
-            dma((9,)), dma((9,)),
-            dma((8,)), dma((8,)),
+            dma((2, NZ, 2)), dma((2, NZ, 2)),
+            dma((2, 8)), dma((2, 8)),
             dma((WCH, 2)), dma((WCH,)), dma((WCH,)), dma((WCH,)), dma, dma, dma, dma,
             dma((NU, 2)), dma((NX, 2, 2)),
             dma((2, 2)), dma((4,)), dma((4,)), dma((4,)),

time: 77.3 us -> 68.7 us (0.89)
  the two profiles are of different devices: /device:TPU:1 before, /device:TPU:3 now
where the time goes in v3:
time: 68.7 us; the launch traced here: 68.4 us
  Pallas kernels  62.7 us (91%)
  local copies, waits for them, and re-layouts  5.61 us (8%)
    pallas_call x1, Pallas kernels, per_device(): pl.pallas_call(kernel, out_shape=jax.ShapeDtypeStruct((rows, d_model // 4...  62.7 us
    unnamed x9, local copies, waits for them, and re-layouts  5.61 us

profile of v3, /device:TPU:3, one launch (start us, length us, event | category | flops | bytes accessed | tf_op | source)
XLA Modules:
  0.0 68.4 jit_solution(17476628015639232032)
XLA Ops:
  0.0 0.0 copy-start
  0.0 2.2 %copy-done = bf16[512,4096]{1,0:T(8,128)(2,1)S(1)} copy-done((bf16[512,4096]{1,0:T(8,128)(2,1)S(1)}, bf16[512,4096]{1,0:T(8,128)(2,1)}, u32[]{:S(2)}) %copy-start) | copy-done | bytes 4194328
  2.2 0.0 copy-start.1
  2.2 0.9 %copy-done.1 = bf16[256,512]{1,0:T(8,128)(2,1)S(1)} copy-done((bf16[256,512]{1,0:T(8,128)(2,1)S(1)}, bf16[256,512]{1,0:T(8,128)(2,1)}, u32[]{:S(2)}) %copy-start.1) | copy-done | bytes 262168
  3.1 0.0 copy-start.2
  3.1 0.8 %copy-done.2 = bf16[256,128]{1,0:T(8,128)(2,1)S(1)} copy-done((bf16[256,128]{1,0:T(8,128)(2,1)S(1)}, bf16[256,128]{1,0:T(8,128)(2,1)}, u32[]{:S(2)}) %copy-start.2) | copy-done | bytes 65560
  4.0 0.0 copy-start.3
  4.0 0.8 %copy-done.3 = bf16[256,128]{1,0:T(8,128)(2,1)S(1)} copy-done((bf16[256,128]{1,0:T(8,128)(2,1)S(1)}, bf16[256,128]{1,0:T(8,128)(2,1)}, u32[]{:S(2)}) %copy-start.3) | copy-done | bytes 65560
  4.8 62.7 %shard_map.46 = bf16[256,1024]{1,0:T(8,128)(2,1)S(1)} custom-call(bf16[256,512]{1,0:T(8,128)(2,1)S(1)} %copy-done.1, bf16[256,128]{1,0:T(8,128)(2,1)S(1)} %copy-done.2, bf16[256,128]{1,0:T(8,128)(2,1)S(1)} %copy-done.3, bf16[512,4096]{1,0:T(8,128)(2,1)S(1)} %copy-done), custom_call_target="tpu_custom_call" | custom-call | tf_op jit(solution)/shard_map/pallas_call | solution.py:587
  67.6 0.8 %copy.6 = bf16[256,1024]{1,0:T(8,128)(2,1)} copy(bf16[256,1024]{1,0:T(8,128)(2,1)S(1)} %shard_map.46) | data formatting | bytes 1048576
Async XLA Ops:
  0.0 2.2 %copy-start = (bf16[512,4096]{1,0:T(8,128)(2,1)S(1)}, bf16[512,4096]{1,0:T(8,128)(2,1)}, u32[]{:S(2)}) copy-start(bf16[512,4096]{1,0:T(8,128)(2,1)} %w_ref.1) | copy-start | bytes 12582916
  2.2 0.9 %copy-start.1 = (bf16[256,512]{1,0:T(8,128)(2,1)S(1)}, bf16[256,512]{1,0:T(8,128)(2,1)}, u32[]{:S(2)}) copy-start(bf16[256,512]{1,0:T(8,128)(2,1)} %q_ref.1) | copy-start | bytes 786436
  3.1 0.8 %copy-start.2 = (bf16[256,128]{1,0:T(8,128)(2,1)S(1)}, bf16[256,128]{1,0:T(8,128)(2,1)}, u32[]{:S(2)}) copy-start(bf16[256,128]{1,0:T(8,128)(2,1)} %k_ref.1) | copy-start | bytes 196612
  4.0 0.8 %copy-start.3 = (bf16[256,128]{1,0:T(8,128)(2,1)S(1)}, bf16[256,128]{1,0:T(8,128)(2,1)}, u32[]{:S(2)}) copy-start(bf16[256,128]{1,0:T(8,128)(2,1)} %v_ref.1) | copy-start | bytes 196612

commit v4 on v3

--- a/solution.py
+++ b/solution.py
@@ -41,7 +41,7 @@
 def kernel(
     q_ref, k_ref, v_ref, w_ref, o_ref,
     vraw, vst, kvbuf, qbuf, s_ref, mx_ref, acc, m_ref, l_ref,
-    osend, ssend, orecv, srecv, attsend, att, wbuf,
+    osend, ssend, orecv, srecv, attsend, att, wbuf, part,
     sw_s, sw_r, qs_s, qs_r, z_s, z_r, sib_s, sib_r,
     w1_s, w1_r, w2_s, w2_r, w3_s, w3_r, wl, vl,
     os_s, os_r, at_s, at_r, as_s, as_r,
@@ -122,8 +122,8 @@
     def q_src(d):
         return q_ref.at[:, pl.ds(d * 2 * HD, 2 * HD)]
 
-    def q_each(remote, local):
-        for i in range(NX):
+    def q_each(remote, local, which=range(NX)):
+        for i in which:
             xt = (col + i) % NX
             for d in range(2):
                 want = jnp.logical_and(low_of(xt) <= mine, jnp.logical_or(xt > 0, mine < NU - 2))
@@ -250,12 +250,18 @@
             for d in range(2):
                 w1(j, d).start()
 
-    q_each(lambda cp: cp.start(), lambda cp: cp.start())
     m_ref[...] = jnp.full_like(m_ref, FLOOR)
     l_ref[...] = jnp.zeros_like(l_ref)
     acc[...] = jnp.zeros_like(acc)
+    @pl.when(jnp.logical_not(stays))
+    def _():
+        kcp.wait_send()
+        vcp.wait_send()
+
+    q_each(lambda cp: cp.start(), lambda cp: cp.start(), (0,))
 
     launch_two(0)
+    q_each(lambda cp: cp.start(), lambda cp: cp.start(), (1, 2, 3))
 
     def q_wait(u):
         pltpu.make_async_copy(qbuf.at[u], qbuf.at[u], qs_r.at[u]).wait()
@@ -387,8 +393,8 @@
             there = xs < x if xs > 0 else jnp.logical_and(x > 0, x < NX - 1)
             pl.when(there)(functools.partial(merge, xs))
         for h in range(2):
-            o = acc[u, :, hs(h)] / l_ref[u, 0:1, hs(h)]
-            attsend[s, :, h * HD:(h + 1) * HD] = o.T.astype(BF)
+            o = acc[u, :, hs(h)] * (1.0 / l_ref[u, 0:1, hs(h)])
+            attsend[s, :, h * HD:(h + 1) * HD] = o.astype(BF).T
         for t in range(2):
             here = owned(s, t)
 
@@ -404,116 +410,102 @@
         w1_in(j).wait_recv()
         w2(j).start()
 
-    def events(seg):
-        if seg == 0:
-            arrive_two()
-            w_on(0)
-            sib_arrive(3)
-        if seg == 1:
-            arrive(1)
-            arrive(2)
-            pl.when(at_end)(functools.partial(launch_one, 1))
-            w_on(1)
-        if seg == 2:
-            sib_arrive(1)
-            sib_arrive(4)
-
-            @pl.when(at_end)
-            def _():
-                arrive_two(1)
-
-            w_on(2)
-        if seg == 3:
-            arrive(5)
-            arrive(6)
-            arrive(7)
-        if seg == 4:
-            for r in (2, 5, 6, 7):
-                sib_arrive(r)
-            w_on(3)
-        if seg == 6:
-            @pl.when(at_end)
-            def _():
-                for r in (1, 2, 5, 6, 7):
-                    arrive(r, 1)
-                for r in range(8):
-                    sib_arrive(r, 1)
-
-    groups = ((0, 3), (1, 4), (2, 5), (6, 7))
-
-    def zpick(k, r0):
-        return jnp.where(k == 0, rel[r0[0]], jnp.where(k == 1, rel[r0[1]], jnp.where(
-            k == 2, rel[r0[2]], rel[r0[3]])))
-
-    def group(k, base):
-        za = zpick(k, [gr[0] for gr in groups])
-        zb = zpick(k, [gr[1] for gr in groups])
-        return [(base, za), (base + 1, za), (base, zb), (base + 1, zb)]
-
     n = top - lo + 1
     far = top - hi
 
-    def pick(seg, *values):
-        out = values[-1]
-        for e in range(len(values) - 2, -1, -1):
-            out = jnp.where(seg == e, values[e], out)
-        return out
-
-    def segment(seg, _):
-        for e in (0, 1, 2, 3, 4, 6):
-            pl.when(seg == e)(functools.partial(events, e))
-        first = pick(seg, 0, n // 2, 0, far // 2, 0, 0, 0)
-        end = pick(seg, n // 2, n, far // 2, far, 2 * far, 6, jnp.where(at_end, 8, 0))
-        count = pick(seg, n, n, far, far, 2 * far, 6, 8)
-        base = jnp.where(seg == 6, 2, 0)
-
-        def at(i):
-            return pick(seg, lo + i, lo + i, hi + 1 + i, hi + 1 + i, top - i // 2,
-                        hi - i // 3, hi - i // 4)
-
-        def grp(i):
-            return group(pick(seg, 0, 0, 1, 1, 2 + i % 2, 1 + i % 3, i % 4), base)
-
-        @pl.when(jnp.logical_and(first == 0, end > 0))
+    def far_end(go, *args):
+        pl.when(at_end)(functools.partial(go, *args))
+
+    def when(cond, *acts):
+        @pl.when(cond)
+        def _():
+            for act in acts:
+                act()
+
+    def each(go, rs, e=0):
+        return lambda: [go(r, e) for r in rs]
+
+    def unit_loop(count, at, blocks, before, after):
+        @pl.when(count > 0)
         def _():
             for h in range(2):
-                score(grp(0), at(0), h)
+                score(blocks(0), at(0), h)
 
         def one(i, _):
             u = at(i)
             nxt = jnp.minimum(i + 1, count - 1)
             un = at(nxt)
-
-            @pl.when(jnp.logical_and(seg < 2, jnp.logical_and(un > u, un > hi)))
-            def _():
-                q_wait(un)
-
+            before(i, u, un)
             for h in range(2):
-                absorb(grp(i), u, grp(nxt), un, h)
-
-            @pl.when(jnp.logical_and(seg == 4, i % 2 == 1))
-            def _():
-                osend[u] = acc[u].astype(BF)
-                lsum = jnp.sum(l_ref[u], axis=0, keepdims=True)
-                ssend[u] = jnp.concatenate(
-                    [jnp.broadcast_to(m_ref[u, 0:1, :], (4, 2 * ROWS)),
-                     jnp.broadcast_to(lsum, (4, 2 * ROWS))], axis=0)
-                o_send(u).start()
-                st_send(u).start()
-
-            complete = jnp.where(at_end, jnp.logical_and(seg == 6, i == 3),
-                                 jnp.logical_and(seg == 5, i == 2))
-
-            @pl.when(complete)
-            def _():
-                finish(1)
-
+                absorb(blocks(i), u, blocks(nxt), un, h)
+            after(i, u)
             return 0
 
-        lax.fori_loop(first, end, one, 0)
+        lax.fori_loop(0, count, one, 0)
+
+    def ring(e, _):
+        base = 2 * e
+        own = e == 0
+        extra = jnp.logical_and(e == 1, at_end)
+        when(own, arrive_two, lambda: w_on(0), each(sib_arrive, (3,)))
+        when(extra, each(arrive, (1, 2), 1), each(sib_arrive, (0, 3), 1))
+
+        def at_first(i):
+            return jnp.where(own, lo + i, hi - i)
+
+        def before_first(i, u, un):
+            when(jnp.logical_and(own, i == n // 2), each(arrive, (1, 2)),
+                 lambda: far_end(launch_one, 1), lambda: w_on(1))
+            when(jnp.logical_and(own, jnp.logical_and(un > u, un > hi)), lambda: q_wait(un))
+
+        few = jnp.where(at_end, 2, 0)
+        unit_loop(jnp.where(own, n, few), at_first,
+                  lambda i: [(base + b, rel[r]) for r in (0, 3) for b in range(2)], before_first, lambda i, u: None)
+
+        def rest(t, _):
+            first = jnp.logical_and(own, t == 0)
+            last = jnp.logical_and(own, t == 1)
+            ends = jnp.logical_and(own, t == 2)
+            when(first, each(sib_arrive, (1, 2, 4)), lambda: far_end(arrive_two, 1), lambda: w_on(2))
+            when(jnp.logical_and(last, far == 0), each(arrive, (5, 6, 7)))
+            when(last, each(sib_arrive, (5, 6, 7)), lambda: pl.when(jnp.logical_not(at_end))(lambda: w_on(3)))
+            when(jnp.logical_and(extra, t == 0), each(sib_arrive, (1, 2, 4), 1))
+            when(jnp.logical_and(extra, t == 1), each(arrive, (5, 6, 7), 1), each(sib_arrive, (5, 6, 7), 1))
+
+            def at(i):
+                return jnp.where(first, hi + 1 + i, jnp.where(last, top - i, jnp.where(ends, hi - i // 2, hi - i)))
+
+            def before(i, u, un):
+                when(jnp.logical_and(first, i == far // 2), each(arrive, (5, 6, 7)))
+                when(jnp.logical_and(ends, jnp.logical_and(at_end, i == 2)), lambda: w_on(3))
+
+            def after(i, u):
+                @pl.when(last)
+                def _():
+                    osend[u] = acc[u].astype(BF)
+                    lsum = jnp.sum(l_ref[u], axis=0, keepdims=True)
+                    ssend[u] = jnp.concatenate(
+                        [jnp.broadcast_to(m_ref[u, 0:1, :], (4, 2 * ROWS)),
+                         jnp.broadcast_to(lsum, (4, 2 * ROWS))], axis=0)
+                    o_send(u).start()
+                    st_send(u).start()
+
+                complete = jnp.where(at_end, jnp.logical_and(jnp.logical_and(extra, t == 1), i == 0),
+                                     jnp.logical_and(ends, i == 1))
+                when(complete, lambda: finish(1))
+
+            def blocks(i):
+                early = jnp.logical_or(t == 0, jnp.logical_and(t == 2, i % 2 == 0))
+                zs = [jnp.where(early, rel[a], rel[b]) for a, b in ((1, 5), (2, 6), (4, 7))]
+                return [(base + b, zz) for zz in zs for b in range(2)]
+
+            unit_loop(jnp.where(t == 2, jnp.where(own, 4, 0), jnp.where(own, far, few)), at, blocks, before, after)
+            return 0
+
+        lax.fori_loop(0, 3, rest, 0)
         return 0
 
-    lax.fori_loop(0, 7, segment, 0)
+    lax.fori_loop(0, 2, ring, 0)
     finish(0)
 
     def a_sib(gg):
@@ -527,19 +519,22 @@
     for j in range(WCH):
         rcopy(wbuf.at[yrow, pl.ds(j * WP, WP), :], wbuf.at[yrow, pl.ds(j * WP, WP), :],
               w2_s.at[j], w2_r.at[j], sib).wait_recv()
+
+    KH = 2 * HD
+
+    def project(core, j):
+        rows = jnp.concatenate([att[i, core] for i in range(4)], axis=1)
+        wcol = jnp.concatenate(
+            [wbuf[i, pl.ds(pl.multiple_of(core * KH, KH), KH), j * 256:(j + 1) * 256] for i in range(4)], axis=0)
+        return jnp.dot(rows, wcol, preferred_element_type=F32)
+
+    for j in range(DC // 256):
+        part[:, j * 256:(j + 1) * 256] = project(c, j)
     for gg in range(4):
         rcopy(att.at[gg, 1 - c], att.at[gg, 1 - c], as_s.at[gg], as_r.at[gg], sib).wait_recv()
-
-    rows = jnp.concatenate([att[i // 2, i % 2] for i in range(8)], axis=1)
     for j in range(DC // 256):
         cs = slice(j * 256, (j + 1) * 256)
-        wcol = jnp.concatenate([wbuf[i, :, cs] for i in range(4)], axis=0)
-        o_ref[:, cs] = jnp.dot(rows, wcol, preferred_element_type=F32).astype(BF)
-
-    @pl.when(jnp.logical_not(stays))
-    def _():
-        kcp.wait_send()
-        vcp.wait_send()
+        o_ref[:, cs] = (part[:, cs] + project(1 - c, j)).astype(BF)
 
     @pl.when(x == 0)
     def _():
@@ -594,7 +589,7 @@
             pltpu.VMEM((ROWS, HD), BF),
             pltpu.VMEM((4, NZ, R2, HD), BF),
             pltpu.VMEM((NU, ROWS, 2 * HD), BF),
-            pltpu.VMEM((4 * ROWS, R2), F32),
+            pltpu.VMEM((6 * ROWS, R2), F32),
             pltpu.VMEM((8, R2), F32),
             pltpu.VMEM((NU, HD, R2), F32),
             pltpu.VMEM((NU, 8, R2), F32),
@@ -606,6 +601,7 @@
             pltpu.VMEM((2, ROWS, 2 * HD), BF),
             pltpu.VMEM((4, 2, ROWS, 2 * HD), BF),
             pltpu.VMEM((4, out_weight.shape[0], d_model // 4), BF),
+            pltpu.VMEM((rows, d_model // 4), F32),
             dma((4,)), dma((4,)),
             dma((NX, 2)), dma((NU,)),
             dma((2, NZ, 2)), dma((2, NZ, 2)),

time: 68.7 us -> 67.7 us (0.985)
  Pallas kernels: 62.7 us -> 61.9 us
    pallas_call x1, Pallas kernels: 62.7 us -> 61.9 us  [per_device(): pl.pallas_call(kernel, out_shape=jax.ShapeDtypeStruct((rows, d_model // 4...]
where the time goes in v4:
time: 67.7 us; the launch traced here: 67.5 us
  Pallas kernels  61.9 us (91%)
  local copies, waits for them, and re-layouts  5.61 us (8%)
    pallas_call x1, Pallas kernels, per_device(): pl.pallas_call(kernel, out_shape=jax.ShapeDtypeStruct((rows, d_model // 4...  61.9 us
    unnamed x9, local copies, waits for them, and re-layouts  5.61 us

profile of v4, /device:TPU:3, one launch (start us, length us, event | category | flops | bytes accessed | tf_op | source)
XLA Modules:
  0.0 67.5 jit_solution(173260847574970774)
XLA Ops:
  0.0 0.0 copy-start
  0.0 2.2 %copy-done = bf16[512,4096]{1,0:T(8,128)(2,1)S(1)} copy-done((bf16[512,4096]{1,0:T(8,128)(2,1)S(1)}, bf16[512,4096]{1,0:T(8,128)(2,1)}, u32[]{:S(2)}) %copy-start) | copy-done | bytes 4194328
  2.2 0.0 copy-start.1
  2.2 0.9 %copy-done.1 = bf16[256,512]{1,0:T(8,128)(2,1)S(1)} copy-done((bf16[256,512]{1,0:T(8,128)(2,1)S(1)}, bf16[256,512]{1,0:T(8,128)(2,1)}, u32[]{:S(2)}) %copy-start.1) | copy-done | bytes 262168
  3.1 0.0 copy-start.2
  3.1 0.8 %copy-done.2 = bf16[256,128]{1,0:T(8,128)(2,1)S(1)} copy-done((bf16[256,128]{1,0:T(8,128)(2,1)S(1)}, bf16[256,128]{1,0:T(8,128)(2,1)}, u32[]{:S(2)}) %copy-start.2) | copy-done | bytes 65560
  4.0 0.0 copy-start.3
  4.0 0.8 %copy-done.3 = bf16[256,128]{1,0:T(8,128)(2,1)S(1)} copy-done((bf16[256,128]{1,0:T(8,128)(2,1)S(1)}, bf16[256,128]{1,0:T(8,128)(2,1)}, u32[]{:S(2)}) %copy-start.3) | copy-done | bytes 65560
  4.8 61.9 %shard_map.46 = bf16[256,1024]{1,0:T(8,128)(2,1)S(1)} custom-call(bf16[256,512]{1,0:T(8,128)(2,1)S(1)} %copy-done.1, bf16[256,128]{1,0:T(8,128)(2,1)S(1)} %copy-done.2, bf16[256,128]{1,0:T(8,128)(2,1)S(1)} %copy-done.3, bf16[512,4096]{1,0:T(8,128)(2,1)S(1)} %copy-done), custom_call_target="tpu_custom_call" | custom-call | tf_op jit(solution)/shard_map/pallas_call | solution.py:582
  66.7 0.8 %copy.6 = bf16[256,1024]{1,0:T(8,128)(2,1)} copy(bf16[256,1024]{1,0:T(8,128)(2,1)S(1)} %shard_map.46) | data formatting | bytes 1048576
Async XLA Ops:
  0.0 2.2 %copy-start = (bf16[512,4096]{1,0:T(8,128)(2,1)S(1)}, bf16[512,4096]{1,0:T(8,128)(2,1)}, u32[]{:S(2)}) copy-start(bf16[512,4096]{1,0:T(8,128)(2,1)} %w_ref.1) | copy-start | bytes 12582916
  2.2 0.9 %copy-start.1 = (bf16[256,512]{1,0:T(8,128)(2,1)S(1)}, bf16[256,512]{1,0:T(8,128)(2,1)}, u32[]{:S(2)}) copy-start(bf16[256,512]{1,0:T(8,128)(2,1)} %q_ref.1) | copy-start | bytes 786436
  3.1 0.8 %copy-start.2 = (bf16[256,128]{1,0:T(8,128)(2,1)S(1)}, bf16[256,128]{1,0:T(8,128)(2,1)}, u32[]{:S(2)}) copy-start(bf16[256,128]{1,0:T(8,128)(2,1)} %k_ref.1) | copy-start | bytes 196612
  4.0 0.8 %copy-start.3 = (bf16[256,128]{1,0:T(8,128)(2,1)S(1)}, bf16[256,128]{1,0:T(8,128)(2,1)}, u32[]{:S(2)}) copy-start(bf16[256,128]{1,0:T(8,128)(2,1)} %v_ref.1) | copy-start | bytes 196612

commit v5 on v4

--- a/solution.py
+++ b/solution.py
@@ -367,11 +367,17 @@
         u = chunk_of(s)
         return jnp.logical_and(u == mine, yh == t)
 
-    def a_remote(s, t):
-        return rcopy(attsend.at[s], att.at[g, c], at_s.at[s, t], at_r.at[g], owner(s, t))
-
-    def a_local(s):
-        return pltpu.make_async_copy(attsend.at[s], att.at[g, c], at_r.at[g])
+    def a_src(s, h):
+        return attsend.at[s, :, pl.ds(h * HD, HD)]
+
+    def a_at(gg, core, h):
+        return att.at[gg, core, :, pl.ds(h * HD, HD)]
+
+    def a_remote(s, t, h):
+        return rcopy(a_src(s, h), a_at(g, c, h), at_s.at[s, t, h], at_r.at[g, h], owner(s, t))
+
+    def a_local(s, h):
+        return pltpu.make_async_copy(a_src(s, h), a_at(g, c, h), at_r.at[g, h])
 
     def finish(s):
         u = chunk_of(s)
@@ -395,16 +401,16 @@
         for h in range(2):
             o = acc[u, :, hs(h)] * (1.0 / l_ref[u, 0:1, hs(h)])
             attsend[s, :, h * HD:(h + 1) * HD] = o.astype(BF).T
-        for t in range(2):
-            here = owned(s, t)
-
-            @pl.when(here)
-            def _():
-                a_local(s).start()
-
-            @pl.when(jnp.logical_not(here))
-            def _():
-                a_remote(s, t).start()
+            for t in range(2):
+                here = owned(s, t)
+
+                @pl.when(here)
+                def _():
+                    a_local(s, h).start()
+
+                @pl.when(jnp.logical_not(here))
+                def _():
+                    a_remote(s, t, h).start()
 
     def w_on(j):
         w1_in(j).wait_recv()
@@ -508,12 +514,13 @@
     lax.fori_loop(0, 2, ring, 0)
     finish(0)
 
-    def a_sib(gg):
-        return rcopy(att.at[gg, c], att.at[gg, c], as_s.at[gg], as_r.at[gg], sib)
-
-    for gg in range(4):
-        pltpu.make_async_copy(attsend.at[0], att.at[gg, c], at_r.at[gg]).wait()
-        a_sib(gg).start()
+    def a_sib(gg, h):
+        return rcopy(a_at(gg, c, h), a_at(gg, c, h), as_s.at[gg, h], as_r.at[gg, h], sib)
+
+    for h in range(2):
+        for gg in range(4):
+            pltpu.make_async_copy(a_src(0, h), a_at(gg, c, h), at_r.at[gg, h]).wait()
+            a_sib(gg, h).start()
     w3.wait_recv()
     wown.wait()
     for j in range(WCH):
@@ -530,8 +537,9 @@
 
     for j in range(DC // 256):
         part[:, j * 256:(j + 1) * 256] = project(c, j)
-    for gg in range(4):
-        rcopy(att.at[gg, 1 - c], att.at[gg, 1 - c], as_s.at[gg], as_r.at[gg], sib).wait_recv()
+    for h in range(2):
+        for gg in range(4):
+            rcopy(a_at(gg, 1 - c, h), a_at(gg, 1 - c, h), as_s.at[gg, h], as_r.at[gg, h], sib).wait_recv()
     for j in range(DC // 256):
         cs = slice(j * 256, (j + 1) * 256)
         o_ref[:, cs] = (part[:, cs] + project(1 - c, j)).astype(BF)
@@ -567,9 +575,11 @@
         for t in range(2):
             @pl.when(jnp.logical_not(owned(s, t)))
             def _():
-                a_remote(s, t).wait_send()
+                for h in range(2):
+                    a_remote(s, t, h).wait_send()
     for gg in range(4):
-        a_sib(gg).wait_send()
+        for h in range(2):
+            a_sib(gg, h).wait_send()
 
 
 def per_device(query, keys, values, out_weight):
@@ -608,7 +618,7 @@
             dma((2, 8)), dma((2, 8)),
             dma((WCH, 2)), dma((WCH,)), dma((WCH,)), dma((WCH,)), dma, dma, dma, dma,
             dma((NU, 2)), dma((NX, 2, 2)),
-            dma((2, 2)), dma((4,)), dma((4,)), dma((4,)),
+            dma((2, 2, 2)), dma((4, 2)), dma((4, 2)), dma((4, 2)),
         ],
         compiler_params=pltpu.CompilerParams(
             collective_id=0, has_side_effects=True, vmem_limit_bytes=48 * 1024 * 1024

time: 67.7 us -> 67.7 us (level)
  no operation moved by 1% of the time
where the time goes in v5:
time: 67.7 us; the launch traced here: 67.4 us
  Pallas kernels  61.8 us (91%)
  local copies, waits for them, and re-layouts  5.61 us (8%)
    pallas_call x1, Pallas kernels, per_device(): pl.pallas_call(kernel, out_shape=jax.ShapeDtypeStruct((rows, d_model // 4...  61.8 us
    unnamed x9, local copies, waits for them, and re-layouts  5.61 us

profile of v5, /device:TPU:3, one launch (start us, length us, event | category | flops | bytes accessed | tf_op | source)
XLA Modules:
  0.0 67.4 jit_solution(17652143927758192250)
XLA Ops:
  0.0 0.0 copy-start
  0.0 2.2 %copy-done = bf16[512,4096]{1,0:T(8,128)(2,1)S(1)} copy-done((bf16[512,4096]{1,0:T(8,128)(2,1)S(1)}, bf16[512,4096]{1,0:T(8,128)(2,1)}, u32[]{:S(2)}) %copy-start) | copy-done | bytes 4194328
  2.2 0.0 copy-start.1
  2.2 0.9 %copy-done.1 = bf16[256,512]{1,0:T(8,128)(2,1)S(1)} copy-done((bf16[256,512]{1,0:T(8,128)(2,1)S(1)}, bf16[256,512]{1,0:T(8,128)(2,1)}, u32[]{:S(2)}) %copy-start.1) | copy-done | bytes 262168
  3.1 0.0 copy-start.2
  3.1 0.8 %copy-done.2 = bf16[256,128]{1,0:T(8,128)(2,1)S(1)} copy-done((bf16[256,128]{1,0:T(8,128)(2,1)S(1)}, bf16[256,128]{1,0:T(8,128)(2,1)}, u32[]{:S(2)}) %copy-start.2) | copy-done | bytes 65560
  4.0 0.0 copy-start.3
  4.0 0.8 %copy-done.3 = bf16[256,128]{1,0:T(8,128)(2,1)S(1)} copy-done((bf16[256,128]{1,0:T(8,128)(2,1)S(1)}, bf16[256,128]{1,0:T(8,128)(2,1)}, u32[]{:S(2)}) %copy-start.3) | copy-done | bytes 65560
  4.8 61.8 %shard_map.46 = bf16[256,1024]{1,0:T(8,128)(2,1)S(1)} custom-call(bf16[256,512]{1,0:T(8,128)(2,1)S(1)} %copy-done.1, bf16[256,128]{1,0:T(8,128)(2,1)S(1)} %copy-done.2, bf16[256,128]{1,0:T(8,128)(2,1)S(1)} %copy-done.3, bf16[512,4096]{1,0:T(8,128)(2,1)S(1)} %copy-done), custom_call_target="tpu_custom_call" | custom-call | tf_op jit(solution)/shard_map/pallas_call | solution.py:592
  66.6 0.8 %copy.6 = bf16[256,1024]{1,0:T(8,128)(2,1)} copy(bf16[256,1024]{1,0:T(8,128)(2,1)S(1)} %shard_map.46) | data formatting | bytes 1048576
Async XLA Ops:
  0.0 2.2 %copy-start = (bf16[512,4096]{1,0:T(8,128)(2,1)S(1)}, bf16[512,4096]{1,0:T(8,128)(2,1)}, u32[]{:S(2)}) copy-start(bf16[512,4096]{1,0:T(8,128)(2,1)} %w_ref.1) | copy-start | bytes 12582916
  2.2 0.9 %copy-start.1 = (bf16[256,512]{1,0:T(8,128)(2,1)S(1)}, bf16[256,512]{1,0:T(8,128)(2,1)}, u32[]{:S(2)}) copy-start(bf16[256,512]{1,0:T(8,128)(2,1)} %q_ref.1) | copy-start | bytes 786436
  3.1 0.8 %copy-start.2 = (bf16[256,128]{1,0:T(8,128)(2,1)S(1)}, bf16[256,128]{1,0:T(8,128)(2,1)}, u32[]{:S(2)}) copy-start(bf16[256,128]{1,0:T(8,128)(2,1)} %k_ref.1) | copy-start | bytes 196612
  4.0 0.8 %copy-start.3 = (bf16[256,128]{1,0:T(8,128)(2,1)S(1)}, bf16[256,128]{1,0:T(8,128)(2,1)}, u32[]{:S(2)}) copy-start(bf16[256,128]{1,0:T(8,128)(2,1)} %v_ref.1) | copy-start | bytes 196612

commit v6 on v5

--- a/solution.py
+++ b/solution.py
@@ -518,7 +518,8 @@
         return rcopy(a_at(gg, c, h), a_at(gg, c, h), as_s.at[gg, h], as_r.at[gg, h], sib)
 
     for h in range(2):
-        for gg in range(4):
+        for away in (0, 1, 3, 2):
+            gg = (g + away) % 4
             pltpu.make_async_copy(a_src(0, h), a_at(gg, c, h), at_r.at[gg, h]).wait()
             a_sib(gg, h).start()
     w3.wait_recv()

time: 67.7 us -> 67.6 us (level)
  no operation moved by 1% of the time
where the time goes in v6:
time: 67.6 us; the launch traced here: 67.3 us
  Pallas kernels  61.7 us (91%)
  local copies, waits for them, and re-layouts  5.61 us (8%)
    pallas_call x1, Pallas kernels, per_device(): pl.pallas_call(kernel, out_shape=jax.ShapeDtypeStruct((rows, d_model // 4...  61.7 us
    unnamed x9, local copies, waits for them, and re-layouts  5.61 us

profile of v6, /device:TPU:3, one launch (start us, length us, event | category | flops | bytes accessed | tf_op | source)
XLA Modules:
  0.0 67.3 jit_solution(572656178831878648)
XLA Ops:
  0.0 0.0 copy-start
  0.0 2.2 %copy-done = bf16[512,4096]{1,0:T(8,128)(2,1)S(1)} copy-done((bf16[512,4096]{1,0:T(8,128)(2,1)S(1)}, bf16[512,4096]{1,0:T(8,128)(2,1)}, u32[]{:S(2)}) %copy-start) | copy-done | bytes 4194328
  2.2 0.0 copy-start.1
  2.2 0.9 %copy-done.1 = bf16[256,512]{1,0:T(8,128)(2,1)S(1)} copy-done((bf16[256,512]{1,0:T(8,128)(2,1)S(1)}, bf16[256,512]{1,0:T(8,128)(2,1)}, u32[]{:S(2)}) %copy-start.1) | copy-done | bytes 262168
  3.1 0.0 copy-start.2
  3.1 0.8 %copy-done.2 = bf16[256,128]{1,0:T(8,128)(2,1)S(1)} copy-done((bf16[256,128]{1,0:T(8,128)(2,1)S(1)}, bf16[256,128]{1,0:T(8,128)(2,1)}, u32[]{:S(2)}) %copy-start.2) | copy-done | bytes 65560
  4.0 0.0 copy-start.3
  4.0 0.8 %copy-done.3 = bf16[256,128]{1,0:T(8,128)(2,1)S(1)} copy-done((bf16[256,128]{1,0:T(8,128)(2,1)S(1)}, bf16[256,128]{1,0:T(8,128)(2,1)}, u32[]{:S(2)}) %copy-start.3) | copy-done | bytes 65560
  4.8 61.7 %shard_map.46 = bf16[256,1024]{1,0:T(8,128)(2,1)S(1)} custom-call(bf16[256,512]{1,0:T(8,128)(2,1)S(1)} %copy-done.1, bf16[256,128]{1,0:T(8,128)(2,1)S(1)} %copy-done.2, bf16[256,128]{1,0:T(8,128)(2,1)S(1)} %copy-done.3, bf16[512,4096]{1,0:T(8,128)(2,1)S(1)} %copy-done), custom_call_target="tpu_custom_call" | custom-call | tf_op jit(solution)/shard_map/pallas_call | solution.py:593
  66.5 0.8 %copy.6 = bf16[256,1024]{1,0:T(8,128)(2,1)} copy(bf16[256,1024]{1,0:T(8,128)(2,1)S(1)} %shard_map.46) | data formatting | bytes 1048576
Async XLA Ops:
  0.0 2.2 %copy-start = (bf16[512,4096]{1,0:T(8,128)(2,1)S(1)}, bf16[512,4096]{1,0:T(8,128)(2,1)}, u32[]{:S(2)}) copy-start(bf16[512,4096]{1,0:T(8,128)(2,1)} %w_ref.1) | copy-start | bytes 12582916
  2.2 0.9 %copy-start.1 = (bf16[256,512]{1,0:T(8,128)(2,1)S(1)}, bf16[256,512]{1,0:T(8,128)(2,1)}, u32[]{:S(2)}) copy-start(bf16[256,512]{1,0:T(8,128)(2,1)} %q_ref.1) | copy-start | bytes 786436
  3.1 0.8 %copy-start.2 = (bf16[256,128]{1,0:T(8,128)(2,1)S(1)}, bf16[256,128]{1,0:T(8,128)(2,1)}, u32[]{:S(2)}) copy-start(bf16[256,128]{1,0:T(8,128)(2,1)} %k_ref.1) | copy-start | bytes 196612
  4.0 0.8 %copy-start.3 = (bf16[256,128]{1,0:T(8,128)(2,1)S(1)}, bf16[256,128]{1,0:T(8,128)(2,1)}, u32[]{:S(2)}) copy-start(bf16[256,128]{1,0:T(8,128)(2,1)} %v_ref.1) | copy-start | bytes 196612
